TPU v7x, 512 devices: a whole 4x4x16 slice. The times are simulated.
512 devices in a mesh: wrap: 32 (over z, y_hi), normal: 16 (over y_lo, x, core).
Axes of the slice: x: 4, y: 4 (y_hi: 2, y_lo: 2; y = y_hi * 2 + y_lo), z: 16, core: 2. Of those that a mesh axis runs over, the one named last changes fastest.
Arguments:
- adjoint_in: bfloat16 [3, 32, 1024, 2048], P(None, None, 'wrap', 'normal'), may hold values from -6 to 6
- coef: float32 [1024, 2048], P('wrap', 'normal'), may hold values from 0.08 to 0.24
- spacing: float32 [1024, 2048], P('wrap', 'normal'), may hold values from 0.5 to 288, as said below
Outputs:
- adjoint_out: bfloat16 [3, 32, 1024, 2048], P(None, None, 'wrap', 'normal')
- wall_sens: float32 [3, 32, 1024], P(None, 'normal', 'wrap')
Inputs may be any that keep to these rules, and one draw needn't show every extreme that they name: `spacing`: positive arc lengths.
All inputs are finite; a program needn't handle non-finite values.
Results may differ from a plain program's by a relative error of at most 0.001.
Values sent between devices are 32-bit elements; how exact they have to be, the bound alone decides.
No kernel may reach another device: no remote copies, remote signals or barrier semaphores. Data moves between devices by JAX's collectives and lax.ppermute only.
A program may use at most 64 MiB of HBM per device.

v0:
```python
import math

import jax
import jax.numpy as jnp
from jax import lax
from jax.sharding import PartitionSpec as P

SWEEPS = 4


def with_halo(cells, sides, width, closed):
    for axis, dim in sides:
        count = lax.axis_size(axis)
        ends = count if closed else count - 1
        head = lax.slice_in_dim(cells, 0, width, axis=dim)
        tail = lax.slice_in_dim(cells, cells.shape[dim] - width, cells.shape[dim], axis=dim)
        cells = jnp.concatenate(
            [
                lax.ppermute(tail, axis, [(i, (i + 1) % count) for i in range(ends)]),
                cells,
                lax.ppermute(head, axis, [((i + 1) % count, i) for i in range(ends)]),
            ],
            axis=dim,
        )
    return cells


def prefix(shard, axis, combine, identity):
    length, place = (lax.axis_size(axis), lax.axis_index(axis))
    everything = lax.all_gather(shard, axis)
    start = jnp.broadcast_to(jnp.asarray(identity, shard.dtype), shard.shape)

    def turn(k, before):
        reached = k < place
        new = combine(before, everything[k])
        return jnp.where(reached, new, before)

    return lax.fori_loop(0, length, turn, start)


def add_terms(earlier, later):
    return earlier + later


def body(adjoint_in, coef, spacing):
    planes = adjoint_in.shape[1]
    wrap_rows, line_cols = coef.shape
    total_cols = line_cols * lax.axis_size("normal")
    first_col = lax.axis_index("normal") * line_cols
    adjoint = adjoint_in.reshape(3 * planes, wrap_rows, line_cols).astype(jnp.float32)
    global_col = first_col + jnp.arange(line_cols)
    interior = ((global_col > 0) & (global_col < total_cols - 1)).astype(jnp.float32)
    factor = coef * interior[None, :]
    for repeat in range(SWEEPS):
        weighted = adjoint * factor[None]
        along_wrap = with_halo(weighted, (("wrap", 1),), 1, True)
        along_normal = with_halo(weighted, (("normal", 2),), 1, False)
        adjoint = (
            adjoint
            + along_wrap[:, 2:]
            + along_wrap[:, :-2]
            + along_normal[:, :, 2:]
            + along_normal[:, :, :-2]
            - 4.0 * weighted
        )
    adjoint_out = adjoint.reshape(3, planes, wrap_rows, line_cols).astype(jnp.bfloat16)
    own_total = jnp.sum(spacing, axis=1)
    line_start = prefix(own_total, "normal", add_terms, jnp.zeros_like(own_total))
    before = line_start[:, None] + jnp.cumsum(spacing, axis=1) - spacing
    root_scale = math.sqrt(total_cols)
    line_total = lax.psum(own_total, "normal")
    weight = (1.0 - before / line_total[:, None]) * spacing / line_total[:, None] * root_scale
    partial_value = jnp.sum(adjoint * weight[None], axis=2).reshape(3, planes, wrap_rows)
    wall_sens = lax.psum_scatter(partial_value, "normal", scatter_dimension=1, tiled=True)
    return (adjoint_out, wall_sens)


def solution(mesh):
    placed = (P(None, None, "wrap", "normal"), P("wrap", "normal"), P("wrap", "normal"))
    return jax.shard_map(
        body,
        mesh=mesh,
        in_specs=placed,
        out_specs=(P(None, None, "wrap", "normal"), P(None, "normal", "wrap")),
        check_vma=False,
    )
```

profile of v0, /device:TPU:8, one launch (start us, length us, event | category | flops | bytes accessed | tf_op | source)
XLA Modules:
  0.0 220.1 jit_solution(13707898314694518733)
XLA Ops:
  0.6 0.7 broadcast_multiply_fusion.3
  1.4 1.3 convert_multiply_fusion
  2.8 13.1 %collective-permute-start = (f32[96,1,128]{2,1,0:T(1,128)S(1)}, f32[96,1,128]{2,1,0:T(1,128)S(1)}, u32[]{:S(2)}, u32[]{:S(2)}) collective-permute-start(f32[96,1,128]{2,1,0:T(1,128)S(1)} %get-tuple-element.129), channel_id=1, source_target_pairs={{16,0},{32,16},{48,32},{64,48},{80,64},{96,80},{112,96},{128,112},... | collective-permute-start | bytes 147464 | tf_op jit(solution)/shard_map/ppermute | solution.py:21
  15.9 1.9 collective-permute-start.1
  17.9 1.8 fusion.30
  19.6 2.2 %copy.9 = f32[96,32,1]{0,1,2:T(8,128)S(1)} copy(f32[96,32,1]{2,1,0:T(8,128)} %get-tuple-element.131) | data formatting | bytes 24576 | tf_op jit(solution)/shard_map/slice | solution.py:15
  21.8 4.6 %collective-permute-start.2 = (f32[96,32,1]{0,1,2:T(8,128)S(1)}, f32[96,32,1]{0,1,2:T(8,128)S(1)}, u32[]{:S(2)}, u32[]{:S(2)}) collective-permute-start(f32[96,32,1]{0,1,2:T(8,128)S(1)} %copy.9), channel_id=1, source_target_pairs={{1,0},{2,1},{3,2},{4,3},{5,4},{6,5},{7,6},{8,7},{9,8},{10,9},{11,1... | collective-permute-start | bytes 36872 | tf_op jit(solution)/shard_map/ppermute | solution.py:21
  26.4 1.0 copy.11
  27.4 1.9 collective-permute-start.3
  29.3 2.3 %copy.10 = f32[96,32,1]{2,1,0:T(8,128)} copy(f32[96,32,1]{0,1,2:T(8,128)S(1)} %collective-permute-done.2) | data formatting | bytes 24576 | tf_op jit(solution)/shard_map/ppermute | solution.py:21
  31.7 2.9 %collective-permute-done.3 = f32[96,32,1]{0,1,2:T(8,128)S(1)} collective-permute-done((f32[96,32,1]{0,1,2:T(8,128)S(1)}, f32[96,32,1]{0,1,2:T(8,128)S(1)}, u32[]{:S(2)}, u32[]{:S(2)}) %collective-permute-start.3) | collective-permute-done | bytes 12320 | tf_op jit(solution)/shard_map/ppermute | solution.py:19
  34.6 2.4 %copy.12 = f32[96,32,1]{2,1,0:T(8,128)} copy(f32[96,32,1]{0,1,2:T(8,128)S(1)} %collective-permute-done.3) | data formatting | bytes 24576 | tf_op jit(solution)/shard_map/ppermute | solution.py:19
  36.9 4.5 %broadcast_multiply_fusion.2 = (f32[96,32,128]{2,1,0:T(8,128)S(1)}, f32[96,32,128]{2,1,0:T(8,128)}) fusion(f32[32,128]{1,0:T(8,128)S(1)} %broadcast_multiply_fusion.3, f32[96,32,128]{2,1,0:T(8,128)S(1)} %convert_multiply_fusion, f32[96,32,1]{2,1,0:T(8,128)} %copy.12, f32[96,32,1]{2,1,0:T(8,128)} %copy.10, f32[96,1,128]{2,1,0:T(1,128)S(1)} %collective-permute-done.1, ...), kind=kLoop, calls=%fused_computation.42 | loop fusion | flops 4718592 | bytes 5644288 | tf_op jit(solution)/shard_map/mul | solution.py:55
  41.5 6.7 %collective-permute-start.4 = (f32[96,1,128]{2,1,0:T(1,128)S(1)}, f32[96,1,128]{2,1,0:T(1,128)S(1)}, u32[]{:S(2)}, u32[]{:S(2)}) collective-permute-start(f32[96,1,128]{2,1,0:T(1,128)S(1)} %get-tuple-element.125), channel_id=1, source_target_pairs={{16,0},{32,16},{48,32},{64,48},{80,64},{96,80},{112,96},{128,112},... | collective-permute-start | bytes 147464 | tf_op jit(solution)/shard_map/ppermute | solution.py:21
  48.2 1.9 collective-permute-start.5
  50.1 1.8 fusion.28
  51.8 2.2 %copy.13 = f32[96,32,1]{0,1,2:T(8,128)S(1)} copy(f32[96,32,1]{2,1,0:T(8,128)} %get-tuple-element.127) | data formatting | bytes 24576 | tf_op jit(solution)/shard_map/slice | solution.py:15
  54.1 3.2 %collective-permute-start.6 = (f32[96,32,1]{0,1,2:T(8,128)S(1)}, f32[96,32,1]{0,1,2:T(8,128)S(1)}, u32[]{:S(2)}, u32[]{:S(2)}) collective-permute-start(f32[96,32,1]{0,1,2:T(8,128)S(1)} %copy.13), channel_id=1, source_target_pairs={{1,0},{2,1},{3,2},{4,3},{5,4},{6,5},{7,6},{8,7},{9,8},{10,9},{11,1... | collective-permute-start | bytes 36872 | tf_op jit(solution)/shard_map/ppermute | solution.py:21
  57.3 1.0 copy.15
  58.2 1.9 collective-permute-start.7
  61.8 31.1 %all-reduce.2 = (f32[32]{0:T(128)S(1)}, f32[512]{0:T(512)S(1)}) all-reduce(f32[32]{0:T(128)S(1)} %reduce_sum.18, f32[512]{0:T(512)S(1)} %dynamic-update-slice), channel_id=1, replica_groups=mesh['wrap'=32,'normal'=16] {'normal'}, use_global_device_ids=true, to_apply=%region_4.5 | all-reduce | flops 544 | bytes 4352 | tf_op jit(solution)/shard_map/psum | solution.py:71
  93.0 2.4 %copy.14 = f32[96,32,1]{2,1,0:T(8,128)} copy(f32[96,32,1]{0,1,2:T(8,128)S(1)} %collective-permute-done.6) | data formatting | bytes 24576 | tf_op jit(solution)/shard_map/ppermute | solution.py:21
  95.4 2.3 %copy.16 = f32[96,32,1]{2,1,0:T(8,128)} copy(f32[96,32,1]{0,1,2:T(8,128)S(1)} %collective-permute-done.7) | data formatting | bytes 24576 | tf_op jit(solution)/shard_map/ppermute | solution.py:19
  97.8 4.8 %broadcast_multiply_fusion.1 = (f32[96,32,128]{2,1,0:T(8,128)S(1)}, f32[96,32,128]{2,1,0:T(8,128)}) fusion(f32[32,128]{1,0:T(8,128)S(1)} %broadcast_multiply_fusion.3, f32[96,32,128]{2,1,0:T(8,128)S(1)} %get-tuple-element.115, f32[96,32,1]{2,1,0:T(8,128)} %copy.16, f32[96,32,1]{2,1,0:T(8,128)} %copy.14, f32[96,1,128]{2,1,0:T(1,128)S(1)} %collective-permute-done.5, ...), kind=kLoop, calls=%fused_computation.41 | loop fusion | flops 4325376 | bytes 6430720 | tf_op jit(solution)/shard_map/mul | solution.py:55
  102.6 1.7 fusion.26
  104.4 2.2 %copy.17 = f32[96,32,1]{0,1,2:T(8,128)S(1)} copy(f32[96,32,1]{2,1,0:T(8,128)} %get-tuple-element.123) | data formatting | bytes 24576 | tf_op jit(solution)/shard_map/slice | solution.py:15
  106.6 1.9 collective-permute-start.10
  108.5 1.0 copy.19
  109.5 2.4 %collective-permute-start.11 = (f32[96,32,1]{0,1,2:T(8,128)S(1)}, f32[96,32,1]{0,1,2:T(8,128)S(1)}, u32[]{:S(2)}, u32[]{:S(2)}) collective-permute-start(f32[96,32,1]{0,1,2:T(8,128)S(1)} %copy.19), channel_id=1, source_target_pairs={{0,1},{1,2},{2,3},{3,4},{4,5},{5,6},{6,7},{7,8},{8,9},{9,10},{10,1... | collective-permute-start | bytes 36872 | tf_op jit(solution)/shard_map/ppermute | solution.py:19
  111.9 6.7 %collective-permute-start.8 = (f32[96,1,128]{2,1,0:T(1,128)S(1)}, f32[96,1,128]{2,1,0:T(1,128)S(1)}, u32[]{:S(2)}, u32[]{:S(2)}) collective-permute-start(f32[96,1,128]{2,1,0:T(1,128)S(1)} %get-tuple-element.121), channel_id=1, source_target_pairs={{16,0},{32,16},{48,32},{64,48},{80,64},{96,80},{112,96},{128,112},... | collective-permute-start | bytes 147464 | tf_op jit(solution)/shard_map/ppermute | solution.py:21
  118.5 1.9 collective-permute-start.9
  120.4 0.7 while.14
  121.4 2.4 %copy.18 = f32[96,32,1]{2,1,0:T(8,128)} copy(f32[96,32,1]{0,1,2:T(8,128)S(1)} %collective-permute-done.10) | data formatting | bytes 24576 | tf_op jit(solution)/shard_map/ppermute | solution.py:21
  123.8 2.3 %copy.20 = f32[96,32,1]{2,1,0:T(8,128)} copy(f32[96,32,1]{0,1,2:T(8,128)S(1)} %collective-permute-done.11) | data formatting | bytes 24576 | tf_op jit(solution)/shard_map/ppermute | solution.py:19
  126.1 2.0 collective-permute-done.9
  128.1 4.8 %broadcast_multiply_fusion = (f32[96,32,128]{2,1,0:T(8,128)S(1)}, f32[96,32,128]{2,1,0:T(8,128)}) fusion(f32[32,128]{1,0:T(8,128)S(1)} %broadcast_multiply_fusion.3, f32[96,32,128]{2,1,0:T(8,128)S(1)} %get-tuple-element.113, f32[96,32,1]{2,1,0:T(8,128)} %copy.20, f32[96,32,1]{2,1,0:T(8,128)} %copy.18, f32[96,1,128]{2,1,0:T(1,128)S(1)} %collective-permute-done.9, ...), kind=kLoop, calls=%fused_computation.40 | loop fusion | flops 4325376 | bytes 6430720 | tf_op jit(solution)/shard_map/mul | solution.py:55
  132.9 1.7 fusion.24
  134.7 2.2 %copy.21 = f32[96,32,1]{0,1,2:T(8,128)S(1)} copy(f32[96,32,1]{2,1,0:T(8,128)} %get-tuple-element.119) | data formatting | bytes 24576 | tf_op jit(solution)/shard_map/slice | solution.py:15
  136.9 4.4 %collective-permute-start.14 = (f32[96,32,1]{0,1,2:T(8,128)S(1)}, f32[96,32,1]{0,1,2:T(8,128)S(1)}, u32[]{:S(2)}, u32[]{:S(2)}) collective-permute-start(f32[96,32,1]{0,1,2:T(8,128)S(1)} %copy.21), channel_id=1, source_target_pairs={{1,0},{2,1},{3,2},{4,3},{5,4},{6,5},{7,6},{8,7},{9,8},{10,9},{11,1... | collective-permute-start | bytes 36872 | tf_op jit(solution)/shard_map/ppermute | solution.py:21
  141.4 1.0 copy.23
  142.3 1.9 collective-permute-start.15
  144.2 5.8 %collective-permute-start.12 = (f32[96,1,128]{2,1,0:T(1,128)S(1)}, f32[96,1,128]{2,1,0:T(1,128)S(1)}, u32[]{:S(2)}, u32[]{:S(2)}) collective-permute-start(f32[96,1,128]{2,1,0:T(1,128)S(1)} %get-tuple-element.117), channel_id=1, source_target_pairs={{16,0},{32,16},{48,32},{64,48},{80,64},{96,80},{112,96},{128,112},... | collective-permute-start | bytes 147464 | tf_op jit(solution)/shard_map/ppermute | solution.py:21
  150.1 2.1 collective-permute-start.13
  153.0 2.3 %copy.22 = f32[96,32,1]{2,1,0:T(8,128)} copy(f32[96,32,1]{0,1,2:T(8,128)S(1)} %collective-permute-done.14) | data formatting | bytes 24576 | tf_op jit(solution)/shard_map/ppermute | solution.py:21
  155.3 2.4 %copy.24 = f32[96,32,1]{2,1,0:T(8,128)} copy(f32[96,32,1]{0,1,2:T(8,128)S(1)} %collective-permute-done.15) | data formatting | bytes 24576 | tf_op jit(solution)/shard_map/ppermute | solution.py:19
  157.7 2.0 collective-permute-done.13
  159.7 4.1 %multiply_reduce_fusion = (f32[96,32]{1,0:T(8,128)S(1)}, bf16[96,32,128]{2,1,0:T(8,128)(2,1)}) fusion(f32[32,128]{1,0:T(8,128)S(1)} %divide_multiply_fusion, f32[96,32,128]{2,1,0:T(8,128)S(1)} %get-tuple-element.111, f32[96,32,1]{2,1,0:T(8,128)} %copy.24, f32[96,32,1]{2,1,0:T(8,128)} %copy.22, f32[96,1,128]{2,1,0:T(1,128)S(1)} %collective-permute-done.13, ...), kind=kLoop, calls=%fused_computation.39 | loop fusion | flops 5108736 | bytes 4083712 | tf_op jit(solution)/shard_map/reduce_sum | solution.py:73
  163.8 55.8 %all-reduce.1 = f32[3,32,32]{2,1,0:T(8,128)S(1)} all-reduce(f32[3,32,32]{2,1,0:T(8,128)S(1)} %bitcast.16), channel_id=3, replica_groups=mesh['wrap'=32,'normal'=16] {'normal'}, use_global_device_ids=true, to_apply=%region_6.7.clone | all-reduce | flops 3072 | bytes 24576
  (49 shorter events, 2.6 us)
Async XLA Ops:
  2.8 34.1 %collective-permute-start = (f32[96,1,128]{2,1,0:T(1,128)S(1)}, f32[96,1,128]{2,1,0:T(1,128)S(1)}, u32[]{:S(2)}, u32[]{:S(2)}) collective-permute-start(f32[96,1,128]{2,1,0:T(1,128)S(1)} %get-tuple-element.129), channel_id=1, source_target_pairs={{16,0},{32,16},{48,32},{64,48},{80,64},{96,80},{112,96},{128,112},... | collective-permute-start | bytes 147464 | tf_op jit(solution)/shard_map/ppermute | solution.py:21
  15.9 21.0 %collective-permute-start.1 = (f32[96,1,128]{2,1,0:T(1,128)S(1)}, f32[96,1,128]{2,1,0:T(1,128)S(1)}, u32[]{:S(2)}, u32[]{:S(2)}) collective-permute-start(f32[96,1,128]{2,1,0:T(1,128)S(1)} %get-tuple-element.130), channel_id=1, source_target_pairs={{0,16},{16,32},{32,48},{48,64},{64,80},{80,96},{96,112},{112,128},... | collective-permute-start | bytes 147464 | tf_op jit(solution)/shard_map/ppermute | solution.py:19
  21.8 7.5 %collective-permute-start.2 = (f32[96,32,1]{0,1,2:T(8,128)S(1)}, f32[96,32,1]{0,1,2:T(8,128)S(1)}, u32[]{:S(2)}, u32[]{:S(2)}) collective-permute-start(f32[96,32,1]{0,1,2:T(8,128)S(1)} %copy.9), channel_id=1, source_target_pairs={{1,0},{2,1},{3,2},{4,3},{5,4},{6,5},{7,6},{8,7},{9,8},{10,9},{11,1... | collective-permute-start | bytes 36872 | tf_op jit(solution)/shard_map/ppermute | solution.py:21
  27.4 7.2 %collective-permute-start.3 = (f32[96,32,1]{0,1,2:T(8,128)S(1)}, f32[96,32,1]{0,1,2:T(8,128)S(1)}, u32[]{:S(2)}, u32[]{:S(2)}) collective-permute-start(f32[96,32,1]{0,1,2:T(8,128)S(1)} %copy.11), channel_id=1, source_target_pairs={{0,1},{1,2},{2,3},{3,4},{4,5},{5,6},{6,7},{7,8},{8,9},{9,10},{10,1... | collective-permute-start | bytes 36872 | tf_op jit(solution)/shard_map/ppermute | solution.py:19
  41.5 56.3 %collective-permute-start.4 = (f32[96,1,128]{2,1,0:T(1,128)S(1)}, f32[96,1,128]{2,1,0:T(1,128)S(1)}, u32[]{:S(2)}, u32[]{:S(2)}) collective-permute-start(f32[96,1,128]{2,1,0:T(1,128)S(1)} %get-tuple-element.125), channel_id=1, source_target_pairs={{16,0},{32,16},{48,32},{64,48},{80,64},{96,80},{112,96},{128,112},... | collective-permute-start | bytes 147464 | tf_op jit(solution)/shard_map/ppermute | solution.py:21
  48.2 49.6 %collective-permute-start.5 = (f32[96,1,128]{2,1,0:T(1,128)S(1)}, f32[96,1,128]{2,1,0:T(1,128)S(1)}, u32[]{:S(2)}, u32[]{:S(2)}) collective-permute-start(f32[96,1,128]{2,1,0:T(1,128)S(1)} %get-tuple-element.126), channel_id=1, source_target_pairs={{0,16},{16,32},{32,48},{48,64},{64,80},{80,96},{96,112},{112,128},... | collective-permute-start | bytes 147464 | tf_op jit(solution)/shard_map/ppermute | solution.py:19
  51.8 8.3 %copy-start.2 = (u32[512]{0:T(512)S(1)}, u32[512]{0:T(512)}, u32[]{:S(2)}) copy-start(u32[512]{0:T(512)} %constant.47) | copy-start | bytes 6148
  51.8 9.6 %copy-start.1 = (f32[32,128]{1,0:T(8,128)S(1)}, f32[32,128]{1,0:T(8,128)}, u32[]{:S(2)}) copy-start(f32[32,128]{1,0:T(8,128)} %param.7) | copy-start | bytes 49156
  54.1 38.9 %collective-permute-start.6 = (f32[96,32,1]{0,1,2:T(8,128)S(1)}, f32[96,32,1]{0,1,2:T(8,128)S(1)}, u32[]{:S(2)}, u32[]{:S(2)}) collective-permute-start(f32[96,32,1]{0,1,2:T(8,128)S(1)} %copy.13), channel_id=1, source_target_pairs={{1,0},{2,1},{3,2},{4,3},{5,4},{6,5},{7,6},{8,7},{9,8},{10,9},{11,1... | collective-permute-start | bytes 36872 | tf_op jit(solution)/shard_map/ppermute | solution.py:21
  58.2 37.2 %collective-permute-start.7 = (f32[96,32,1]{0,1,2:T(8,128)S(1)}, f32[96,32,1]{0,1,2:T(8,128)S(1)}, u32[]{:S(2)}, u32[]{:S(2)}) collective-permute-start(f32[96,32,1]{0,1,2:T(8,128)S(1)} %copy.15), channel_id=1, source_target_pairs={{0,1},{1,2},{2,3},{3,4},{4,5},{5,6},{6,7},{7,8},{8,9},{9,10},{10,1... | collective-permute-start | bytes 36872 | tf_op jit(solution)/shard_map/ppermute | solution.py:19
  106.6 14.8 %collective-permute-start.10 = (f32[96,32,1]{0,1,2:T(8,128)S(1)}, f32[96,32,1]{0,1,2:T(8,128)S(1)}, u32[]{:S(2)}, u32[]{:S(2)}) collective-permute-start(f32[96,32,1]{0,1,2:T(8,128)S(1)} %copy.17), channel_id=1, source_target_pairs={{1,0},{2,1},{3,2},{4,3},{5,4},{6,5},{7,6},{8,7},{9,8},{10,9},{11,1... | collective-permute-start | bytes 36872 | tf_op jit(solution)/shard_map/ppermute | solution.py:21
  109.5 14.3 %collective-permute-start.11 = (f32[96,32,1]{0,1,2:T(8,128)S(1)}, f32[96,32,1]{0,1,2:T(8,128)S(1)}, u32[]{:S(2)}, u32[]{:S(2)}) collective-permute-start(f32[96,32,1]{0,1,2:T(8,128)S(1)} %copy.19), channel_id=1, source_target_pairs={{0,1},{1,2},{2,3},{3,4},{4,5},{5,6},{6,7},{7,8},{8,9},{9,10},{10,1... | collective-permute-start | bytes 36872 | tf_op jit(solution)/shard_map/ppermute | solution.py:19
  111.9 14.3 %collective-permute-start.8 = (f32[96,1,128]{2,1,0:T(1,128)S(1)}, f32[96,1,128]{2,1,0:T(1,128)S(1)}, u32[]{:S(2)}, u32[]{:S(2)}) collective-permute-start(f32[96,1,128]{2,1,0:T(1,128)S(1)} %get-tuple-element.121), channel_id=1, source_target_pairs={{16,0},{32,16},{48,32},{64,48},{80,64},{96,80},{112,96},{128,112},... | collective-permute-start | bytes 147464 | tf_op jit(solution)/shard_map/ppermute | solution.py:21
  118.5 9.6 %collective-permute-start.9 = (f32[96,1,128]{2,1,0:T(1,128)S(1)}, f32[96,1,128]{2,1,0:T(1,128)S(1)}, u32[]{:S(2)}, u32[]{:S(2)}) collective-permute-start(f32[96,1,128]{2,1,0:T(1,128)S(1)} %get-tuple-element.122), channel_id=1, source_target_pairs={{0,16},{16,32},{32,48},{48,64},{64,80},{80,96},{96,112},{112,128},... | collective-permute-start | bytes 147464 | tf_op jit(solution)/shard_map/ppermute | solution.py:19
  136.9 16.1 %collective-permute-start.14 = (f32[96,32,1]{0,1,2:T(8,128)S(1)}, f32[96,32,1]{0,1,2:T(8,128)S(1)}, u32[]{:S(2)}, u32[]{:S(2)}) collective-permute-start(f32[96,32,1]{0,1,2:T(8,128)S(1)} %copy.21), channel_id=1, source_target_pairs={{1,0},{2,1},{3,2},{4,3},{5,4},{6,5},{7,6},{8,7},{9,8},{10,9},{11,1... | collective-permute-start | bytes 36872 | tf_op jit(solution)/shard_map/ppermute | solution.py:21
  142.3 13.0 %collective-permute-start.15 = (f32[96,32,1]{0,1,2:T(8,128)S(1)}, f32[96,32,1]{0,1,2:T(8,128)S(1)}, u32[]{:S(2)}, u32[]{:S(2)}) collective-permute-start(f32[96,32,1]{0,1,2:T(8,128)S(1)} %copy.23), channel_id=1, source_target_pairs={{0,1},{1,2},{2,3},{3,4},{4,5},{5,6},{6,7},{7,8},{8,9},{9,10},{10,1... | collective-permute-start | bytes 36872 | tf_op jit(solution)/shard_map/ppermute | solution.py:19
  144.2 13.5 %collective-permute-start.12 = (f32[96,1,128]{2,1,0:T(1,128)S(1)}, f32[96,1,128]{2,1,0:T(1,128)S(1)}, u32[]{:S(2)}, u32[]{:S(2)}) collective-permute-start(f32[96,1,128]{2,1,0:T(1,128)S(1)} %get-tuple-element.117), channel_id=1, source_target_pairs={{16,0},{32,16},{48,32},{64,48},{80,64},{96,80},{112,96},{128,112},... | collective-permute-start | bytes 147464 | tf_op jit(solution)/shard_map/ppermute | solution.py:21
  150.1 9.6 %collective-permute-start.13 = (f32[96,1,128]{2,1,0:T(1,128)S(1)}, f32[96,1,128]{2,1,0:T(1,128)S(1)}, u32[]{:S(2)}, u32[]{:S(2)}) collective-permute-start(f32[96,1,128]{2,1,0:T(1,128)S(1)} %get-tuple-element.118), channel_id=1, source_target_pairs={{0,16},{16,32},{32,48},{48,64},{64,80},{80,96},{96,112},{112,128},... | collective-permute-start | bytes 147464 | tf_op jit(solution)/shard_map/ppermute | solution.py:19
  153.0 6.8 %copy-start = (f32[96,32,128]{2,1,0:T(8,128)S(1)}, f32[96,32,128]{2,1,0:T(8,128)}, u32[]{:S(2)}) copy-start(f32[96,32,128]{2,1,0:T(8,128)} %get-tuple-element.112) | copy-start | bytes 4718596
where the time goes:
time: 221 us; the launch traced here: 220 us
  blocking collectives  86.9 us (39%)
  starting transfers between devices  62.4 us (28%)
  local copies, waits for them, and re-layouts  40.3 us (18%)
  other arithmetic  21 us (10%)
  waiting for transfers between devices  6.91 us (3%)
  between operations  2.21 us (1%)
    unnamed x1, blocking collectives  55.8 us
    ppermute x8, starting transfers between devices, with_halo(): lax.ppermute(head, axis, [((i + 1) % count, i) for i in range(ends)])  46.4 us
    psum x1, blocking collectives, body(): line_total = lax.psum(own_total, 'normal')  31.1 us
    slice x12, local copies, waits for them, and re-layouts, with_halo(): head = lax.slice_in_dim(cells, 0, width, axis=dim)  16.1 us
    ppermute x8, starting transfers between devices, with_halo(): lax.ppermute(tail, axis, [(i, (i + 1) % count) for i in range(ends)])  16 us
    mul x4, other arithmetic, body(): weighted = adjoint * factor[None]  15.4 us
    ppermute x4, local copies, waits for them, and re-layouts, with_halo(): lax.ppermute(head, axis, [((i + 1) % count, i) for i in range(ends)])  9.47 us
    ppermute x4, local copies, waits for them, and re-layouts, with_halo(): lax.ppermute(tail, axis, [(i, (i + 1) % count) for i in range(ends)])  9.41 us
  transfers between devices with their start and end apart: 16, of which 3 were waited for; matrix products, arithmetic and copies ran while one was open for 15% of the time, Pallas kernels for 0%

commit v1 on v0

v1 whole, which is shorter than its diff:
```python
import math

import jax
import jax.numpy as jnp
from jax import lax
from jax.experimental import pallas as pl
from jax.experimental.pallas import tpu as pltpu
from jax.sharding import PartitionSpec as P

SWEEPS = 4
HALO = 4
PLANES = 96
ROWS = 32
COLS = 128
ALL_ROWS = ROWS + 2 * HALO
ALL_COLS = COLS + 2 * HALO
MSG = HALO * PLANES + HALO * 2 * HALO + 8
F32 = jnp.float32
BF16 = jnp.bfloat16
VMEM = pl.BlockSpec(memory_space=pltpu.VMEM)


def nt(a, b):
    return lax.dot_general(a, b, (((1,), (1,)), ((), ())), preferred_element_type=F32)


def iota(shape, dim):
    return lax.broadcasted_iota(jnp.int32, shape, dim)


def call(kernel, outs, scratch, cost):
    single = not isinstance(outs, (list, tuple))
    return pl.pallas_call(
        kernel,
        out_shape=outs,
        out_specs=VMEM if single else [VMEM] * len(outs),
        scratch_shapes=scratch,
        compiler_params=pltpu.CompilerParams(vmem_limit_bytes=40 * 1024 * 1024),
        cost_estimate=pl.CostEstimate(flops=cost, bytes_accessed=2_000_000, transcendentals=0),
    )


def edge_kernel(x_ref, coef_ref, left_ref, right_ref, top_ref, bottom_ref, xf):
    xf[...] = x_ref[...].astype(F32).reshape(PLANES * ROWS, COLS)
    row, col = iota((2 * HALO, COLS), 0), iota((2 * HALO, COLS), 1)
    pick = (col == jnp.where(row < HALO, row, COLS - 2 * HALO + row)).astype(BF16)
    coef = coef_ref[...]
    coef_t = jnp.transpose(coef)
    ends = jnp.concatenate([coef_t[:HALO], coef_t[COLS - HALO :]], axis=0)
    pad = jnp.zeros((COLS - PLANES, COLS), BF16)
    lane = iota((2 * HALO, COLS), 1)
    for i in range(ROWS):
        planes = xf[pl.ds(i, PLANES, stride=ROWS), :]
        strip = nt(pick, jnp.concatenate([planes.astype(BF16), pad], axis=0))
        strip = jnp.where(lane < PLANES, strip, jnp.broadcast_to(ends[:, i : i + 1], (2 * HALO, COLS)))
        left_ref[i] = strip[:HALO]
        right_ref[i] = strip[HALO:]
        if i < HALO:
            top_ref[pl.ds(i * PLANES, PLANES), :] = planes
        if i >= ROWS - HALO:
            bottom_ref[pl.ds((i - ROWS + HALO) * PLANES, PLANES), :] = planes
    zero = jnp.zeros((HALO, COLS), F32)
    top_ref[pl.ds(MSG - 8, 8), :] = jnp.concatenate([coef[:HALO], zero], axis=0)
    bottom_ref[pl.ds(MSG - 8, 8), :] = jnp.concatenate([coef[ROWS - HALO :], zero], axis=0)
    for ref in (top_ref, bottom_ref):
        ref[pl.ds(HALO * PLANES, 8 * HALO), :] = jnp.zeros((8 * HALO, COLS), F32)


def corner_kernel(from_left, from_right, top_in, bottom_in, top_ref, bottom_ref):
    top_ref[...] = top_in[...]
    bottom_ref[...] = bottom_in[...]
    for r in range(HALO):
        at = HALO * PLANES + 8 * r
        for ref, i in ((top_ref, r), (bottom_ref, ROWS - HALO + r)):
            ref[pl.ds(at, 8), :] = jnp.concatenate([from_right[i], from_left[i]], axis=0)


def split(value):
    high = value.astype(BF16).astype(F32)
    return high, value - high


def main_kernel(x_ref, coef_ref, spacing_ref, from_left, from_right, above, below, out_ref, sums_ref, xf, v, f, sums):
    place = lax.axis_index("normal")
    last = lax.axis_size("normal") - 1
    xf[...] = x_ref[...].astype(F32).reshape(PLANES * ROWS, COLS)
    eye = (iota((COLS, COLS), 0) == iota((COLS, COLS), 1)).astype(BF16)
    pad = jnp.zeros((COLS - PLANES, COLS), BF16)
    at = HALO * PLANES + 8 * HALO
    coef_all = jnp.concatenate(
        [above[pl.ds(at, HALO), :], coef_ref[...], below[pl.ds(at, HALO), :], jnp.zeros((COLS - ALL_ROWS, COLS), F32)],
        axis=0,
    )
    coef_t = jnp.transpose(coef_all)
    own_col = iota((COLS, COLS), 0)
    inside = jnp.logical_not(((own_col == 0) & (place == 0)) | ((own_col == COLS - 1) & (place == last)))
    coef_t = jnp.where(inside, coef_t, 0.0)
    for r in range(ALL_ROWS):
        if r < HALO:
            planes = above[pl.ds(r * PLANES, PLANES), :]
            strip = above[pl.ds(HALO * PLANES + 8 * r, 8), :]
        elif r < HALO + ROWS:
            planes = xf[pl.ds(r - HALO, PLANES, stride=ROWS), :]
            strip = jnp.concatenate([from_right[r - HALO], from_left[r - HALO]], axis=0)
        else:
            k = r - HALO - ROWS
            planes = below[pl.ds(k * PLANES, PLANES), :]
            strip = below[pl.ds(HALO * PLANES + 8 * k, 8), :]
        v[r, pl.ds(0, COLS), :] = nt(eye, jnp.concatenate([planes.astype(BF16), pad], axis=0))
        v[r, pl.ds(COLS, 8), :] = strip
        f[r, pl.ds(0, COLS), :] = jnp.broadcast_to(coef_t[:, r : r + 1], (COLS, COLS))
        f[r, pl.ds(COLS, 8), :] = jnp.broadcast_to(strip[:, PLANES : PLANES + 1], (8, COLS))

    for sweep in range(SWEEPS):

        def update(r, held):
            before, here = held
            after = f[r + 1] * v[r + 1]
            beside = pltpu.roll(here, 1, 0) + pltpu.roll(here, ALL_COLS - 1, 0)
            v[r] = (v[r] - 4.0 * here) + ((before + after) + beside)
            return here, after

        lax.fori_loop(sweep + 1, ALL_ROWS - 1 - sweep, update, (f[sweep] * v[sweep], f[sweep + 1] * v[sweep + 1]))

    spacing = spacing_ref[...]
    earlier = (iota((COLS, COLS), 0) < iota((COLS, COLS), 1)).astype(F32)
    before = lax.dot_general(
        spacing, earlier, (((1,), (0,)), ((), ())), preferred_element_type=F32, precision=lax.Precision.HIGHEST
    )
    s_high, s_low = split(spacing)
    q_high, q_low = split(before * spacing)
    sums[pl.ds(2 * ROWS, ROWS), :] = jnp.broadcast_to(jnp.sum(spacing, axis=1, keepdims=True), (ROWS, COLS))
    sums[pl.ds(3 * ROWS, ROWS), :] = jnp.zeros((ROWS, COLS), F32)
    place16 = iota((16, COLS), 0)
    for i in range(ROWS):
        value = v[HALO + i, pl.ds(0, COLS), :]
        high = value.astype(BF16)
        low = (value - high.astype(F32)).astype(BF16)
        rows = [jnp.broadcast_to(a[i : i + 1], (16, COLS)) for a in (s_high, q_high, s_low, q_low)]
        weight = jnp.where(
            place16 == 0,
            rows[0],
            jnp.where(place16 == 1, rows[1], jnp.where(place16 == 2, rows[2], jnp.where(place16 == 3, rows[3], 0.0))),
        ).astype(BF16)
        both = lax.dot_general(weight, high, (((1,), (0,)), ((), ())), preferred_element_type=F32) + lax.dot_general(
            weight, low, (((1,), (0,)), ((), ())), preferred_element_type=F32
        )
        sums[pl.ds(i, 1), :] = both[0:1] + both[2:3]
        sums[pl.ds(ROWS + i, 1), :] = both[1:2] + both[3:4]
        xf[pl.ds(i, PLANES, stride=ROWS), :] = nt(eye[:PLANES], high)
    out_ref[...] = xf[...].astype(BF16).reshape(PLANES, ROWS, COLS)
    sums[...] = jnp.transpose(sums[...])
    owners = sums_ref.shape[0]
    each = ROWS // owners
    for c in range(3):
        for e in range(each):
            sums_ref[:, c * each + e, :] = sums[pl.ds(c * ROWS + e, owners, stride=each), :]
    sums_ref[:, 3 * each :, :] = jnp.zeros((owners, 8 - 3 * each, COLS), F32)


def owner_kernel(got_ref, out_ref):
    owners = got_ref.shape[0]
    each = ROWS // owners
    own = [pltpu.roll(got_ref[d], COLS - 2 * ROWS, 1) for d in range(owners)]
    total = own[0]
    for d in range(1, owners):
        total = total + own[d]
    rest = total
    acc = jnp.zeros_like(total)
    moment = jnp.zeros_like(total)
    for d in range(owners):
        acc = acc + got_ref[d] * rest
        moment = moment + got_ref[d]
        rest = rest - own[d]
    acc = acc - pltpu.roll(moment, COLS - ROWS, 1)
    value = (acc / total) / total * math.sqrt(COLS * owners)
    for c in range(3):
        out_ref[c] = value[c * each : (c + 1) * each, :ROWS]


def body(adjoint_in, coef, spacing):
    wraps, owners = lax.axis_size("wrap"), lax.axis_size("normal")
    x = adjoint_in.reshape(PLANES, ROWS, COLS)
    strip = jax.ShapeDtypeStruct((ROWS, HALO, COLS), F32)
    message = jax.ShapeDtypeStruct((MSG, COLS), F32)
    left, right, top, bottom = call(
        edge_kernel, [strip, strip, message, message], [pltpu.VMEM((PLANES * ROWS, COLS), F32)], 10_000_000
    )(x, coef)
    from_left = lax.ppermute(right, "normal", [(k, k + 1) for k in range(owners - 1)])
    from_right = lax.ppermute(left, "normal", [(k + 1, k) for k in range(owners - 1)])
    top, bottom = call(corner_kernel, [message, message], [], 1_000_000)(from_left, from_right, top, bottom)
    above = lax.ppermute(bottom, "wrap", [(k, (k + 1) % wraps) for k in range(wraps)])
    below = lax.ppermute(top, "wrap", [((k + 1) % wraps, k) for k in range(wraps)])
    adjoint_out, sums = call(
        main_kernel,
        [jax.ShapeDtypeStruct((PLANES, ROWS, COLS), BF16), jax.ShapeDtypeStruct((owners, 8, COLS), F32)],
        [
            pltpu.VMEM((PLANES * ROWS, COLS), F32),
            pltpu.VMEM((ALL_ROWS, ALL_COLS, COLS), F32),
            pltpu.VMEM((ALL_ROWS, ALL_COLS, COLS), F32),
            pltpu.VMEM((COLS, COLS), F32),
        ],
        50_000_000,
    )(x, coef, spacing, from_left, from_right, above, below)
    got = lax.all_to_all(sums, "normal", 0, 0, tiled=True)
    wall_sens = call(owner_kernel, jax.ShapeDtypeStruct((3, ROWS // owners, ROWS), F32), [], 100_000)(got)
    return adjoint_out.reshape(3, PLANES // 3, ROWS, COLS), wall_sens


def solution(mesh):
    placed = (P(None, None, "wrap", "normal"), P("wrap", "normal"), P("wrap", "normal"))
    return jax.shard_map(
        body,
        mesh=mesh,
        in_specs=placed,
        out_specs=(P(None, None, "wrap", "normal"), P(None, "normal", "wrap")),
        check_vma=False,
    )
```

time: 221 us -> 54.7 us (0.25)
  the two profiles are of different devices: /device:TPU:8 before, /device:TPU:1 now
where the time goes in v1:
time: 54.7 us; the launch traced here: 54.3 us
  starting transfers between devices  24.9 us (46%)
  blocking collectives  11.4 us (21%)
  Pallas kernels  11.3 us (21%)
  waiting for transfers between devices  4.09 us (7%)
  local copies, waits for them, and re-layouts  1.85 us (3%)
  between operations  0.69 us (1%)
    all_to_all x1, blocking collectives, body(): got = lax.all_to_all(sums, 'normal', 0, 0, tiled=True)  11.4 us
    ppermute x1, starting transfers between devices, body(): lax.ppermute(top, 'wrap', [((k + 1) % wraps, k) for k in range(wraps)])  10.9 us
    pallas_call x1, Pallas kernels, body(): call(main_kernel, [jax.ShapeDtypeStruct((PLANES, ROWS, COLS), BF16), jax....  9.54 us
    ppermute x1, starting transfers between devices, body(): lax.ppermute(left, 'normal', [(k + 1, k) for k in range(owners - 1)])  5.57 us
    ppermute x1, starting transfers between devices, body(): lax.ppermute(right, 'normal', [(k, k + 1) for k in range(owners - 1)])  4.51 us
    ppermute x1, starting transfers between devices, body(): lax.ppermute(bottom, 'wrap', [(k, (k + 1) % wraps) for k in range(wraps)])  3.95 us
    unnamed x10, local copies, waits for them, and re-layouts  1.85 us
    ppermute x1, waiting for transfers between devices, body(): lax.ppermute(top, 'wrap', [((k + 1) % wraps, k) for k in range(wraps)])  1.7 us
  transfers between devices with their start and end apart: 4, of which 3 were waited for; matrix products, arithmetic and copies ran while one was open for 0% of the time, Pallas kernels for 0%

profile of v1, /device:TPU:1, one launch (start us, length us, event | category | flops | bytes accessed | tf_op | source)
XLA Modules:
  0.0 54.3 jit_solution(15959551697664788859)
XLA Ops:
  0.6 0.0 copy-start
  0.6 1.1 %copy-done = bf16[3,32,32,128]{3,2,1,0:T(8,128)(2,1)S(1)} copy-done((bf16[3,32,32,128]{3,2,1,0:T(8,128)(2,1)S(1)}, bf16[3,32,32,128]{3,2,1,0:T(8,128)(2,1)}, u32[]{:S(2)}) %copy-start) | copy-done | bytes 786456
  1.8 0.0 copy-start.2
  1.8 0.7 %copy-done.2 = f32[32,128]{1,0:T(8,128)S(1)} copy-done((f32[32,128]{1,0:T(8,128)S(1)}, f32[32,128]{1,0:T(8,128)}, u32[]{:S(2)}) %copy-start.2) | copy-done | bytes 16408
  2.5 0.0 copy-start.1
  2.5 1.1 %shard_map.50 = (f32[32,4,128]{2,1,0:T(4,128)S(1)}, f32[32,4,128]{2,1,0:T(4,128)S(1)}, f32[424,128]{1,0:T(8,128)S(1)}, f32[424,128]{1,0:T(8,128)S(1)}) custom-call(bf16[96,32,128]{2,1,0:T(8,128)(2,1)S(1)} %bitcast.2, f32[32,128]{1,0:T(8,128)S(1)} %copy-done.2), custom_call_target="tpu_custom_call" | custom-call | flops 10000000 | bytes 2000000 | tf_op jit(solution)/shard_map/pallas_call | solution.py:186
  3.6 4.5 %collective-permute-start = (f32[32,4,128]{2,1,0:T(4,128)S(1)}, f32[32,4,128]{2,1,0:T(4,128)S(1)}, u32[]{:S(2)}, u32[]{:S(2)}) collective-permute-start(f32[32,4,128]{2,1,0:T(4,128)S(1)} %get-tuple-element.10), channel_id=1, source_target_pairs={{0,1},{1,2},{2,3},{3,4},{4,5},{5,6},{6,7},{7,8},{8,9},{9,10},{10,1... | collective-permute-start | bytes 196616 | tf_op jit(solution)/shard_map/ppermute | solution.py:189
  8.1 5.6 %collective-permute-start.1 = (f32[32,4,128]{2,1,0:T(4,128)S(1)}, f32[32,4,128]{2,1,0:T(4,128)S(1)}, u32[]{:S(2)}, u32[]{:S(2)}) collective-permute-start(f32[32,4,128]{2,1,0:T(4,128)S(1)} %get-tuple-element.11), channel_id=1, source_target_pairs={{1,0},{2,1},{3,2},{4,3},{5,4},{6,5},{7,6},{8,7},{9,8},{10,9},{11,1... | collective-permute-start | bytes 196616 | tf_op jit(solution)/shard_map/ppermute | solution.py:190
  13.7 0.0 collective-permute-done.from_left
  13.7 0.9 %collective-permute-done.1.from_right = f32[32,4,128]{2,1,0:T(4,128)S(1)} collective-permute-done((f32[32,4,128]{2,1,0:T(4,128)S(1)}, f32[32,4,128]{2,1,0:T(4,128)S(1)}, u32[]{:S(2)}, u32[]{:S(2)}) %collective-permute-start.1) | collective-permute-done | bytes 65568 | tf_op jit(solution)/shard_map/ppermute | solution.py:190
  14.5 0.0 copy-start.3
  14.5 0.0 copy-start.4
  14.6 3.9 %collective-permute-start.2 = (f32[424,128]{1,0:T(8,128)S(1)}, f32[424,128]{1,0:T(8,128)S(1)}, u32[]{:S(2)}, u32[]{:S(2)}) collective-permute-start(f32[424,128]{1,0:T(8,128)S(1)} %get-tuple-element.14), channel_id=1, source_target_pairs={{0,16},{16,32},{32,48},{48,64},{64,80},{80,96},{96,112},{112,128},... | collective-permute-start | bytes 651272 | tf_op jit(solution)/shard_map/ppermute | solution.py:192
  18.5 10.9 %collective-permute-start.3 = (f32[424,128]{1,0:T(8,128)S(1)}, f32[424,128]{1,0:T(8,128)S(1)}, u32[]{:S(2)}, u32[]{:S(2)}) collective-permute-start(f32[424,128]{1,0:T(8,128)S(1)} %get-tuple-element.15), channel_id=1, source_target_pairs={{16,0},{32,16},{48,32},{64,48},{80,64},{96,80},{112,96},{128,112},... | collective-permute-start | bytes 651272 | tf_op jit(solution)/shard_map/ppermute | solution.py:193
  29.4 1.5 %collective-permute-done.2.above = f32[424,128]{1,0:T(8,128)S(1)} collective-permute-done((f32[424,128]{1,0:T(8,128)S(1)}, f32[424,128]{1,0:T(8,128)S(1)}, u32[]{:S(2)}, u32[]{:S(2)}) %collective-permute-start.2) | collective-permute-done | bytes 217120 | tf_op jit(solution)/shard_map/ppermute | solution.py:192
  30.9 1.7 %collective-permute-done.3.below = f32[424,128]{1,0:T(8,128)S(1)} collective-permute-done((f32[424,128]{1,0:T(8,128)S(1)}, f32[424,128]{1,0:T(8,128)S(1)}, u32[]{:S(2)}, u32[]{:S(2)}) %collective-permute-start.3) | collective-permute-done | bytes 217120 | tf_op jit(solution)/shard_map/ppermute | solution.py:193
  32.6 0.0 copy-done.1
  32.6 0.0 copy-done.3
  32.6 0.0 copy-done.4
  32.6 9.5 %shard_map.52 = (bf16[96,32,128]{2,1,0:T(8,128)(2,1)}, f32[16,8,128]{2,1,0:T(8,128)S(1)}) custom-call(bf16[96,32,128]{2,1,0:T(8,128)(2,1)S(1)} %bitcast.3, f32[32,128]{1,0:T(8,128)S(1)} %copy-done.3, f32[32,128]{1,0:T(8,128)S(1)} %copy-done.4, f32[32,4,128]{2,1,0:T(4,128)S(1)} %collective-permute-done.from_left, ...), custom_call_target="tpu_custom_call" | custom-call | flops 50000000 | bytes 2000000 | tf_op jit(solution)/shard_map/pallas_call | solution.py:194
  42.2 11.4 %all_to_all.5.got_ref = f32[16,8,128]{2,1,0:T(8,128)S(1)} all-to-all(f32[16,8,128]{2,1,0:T(8,128)S(1)} %get-tuple-element.17), channel_id=1, replica_groups=mesh['wrap'=32,'normal'=16] {'normal'}, dimensions={0} | all-to-all | bytes 131072 | tf_op jit(solution)/shard_map/all_to_all | solution.py:205
  53.6 0.7 %shard_map.53 = f32[3,2,32]{2,1,0:T(2,128)} custom-call(f32[16,8,128]{2,1,0:T(8,128)S(1)} %all_to_all.5.got_ref), custom_call_target="tpu_custom_call" | custom-call | flops 100000 | bytes 2000000 | tf_op jit(solution)/shard_map/pallas_call | solution.py:206
  (1 shorter events, 0.0 us)
Async XLA Ops:
  0.6 1.1 %copy-start = (bf16[3,32,32,128]{3,2,1,0:T(8,128)(2,1)S(1)}, bf16[3,32,32,128]{3,2,1,0:T(8,128)(2,1)}, u32[]{:S(2)}) copy-start(bf16[3,32,32,128]{3,2,1,0:T(8,128)(2,1)} %param.3) | copy-start | bytes 2359300
  1.8 0.7 %copy-start.2 = (f32[32,128]{1,0:T(8,128)S(1)}, f32[32,128]{1,0:T(8,128)}, u32[]{:S(2)}) copy-start(f32[32,128]{1,0:T(8,128)} %coef_ref.3) | copy-start | bytes 49156
  2.5 30.1 %copy-start.1 = (bf16[3,32,32,128]{3,2,1,0:T(8,128)(2,1)S(1)}, bf16[3,32,32,128]{3,2,1,0:T(8,128)(2,1)}, u32[]{:S(2)}) copy-start(bf16[3,32,32,128]{3,2,1,0:T(8,128)(2,1)} %param.3) | copy-start | bytes 2359300
  3.6 10.1 %collective-permute-start = (f32[32,4,128]{2,1,0:T(4,128)S(1)}, f32[32,4,128]{2,1,0:T(4,128)S(1)}, u32[]{:S(2)}, u32[]{:S(2)}) collective-permute-start(f32[32,4,128]{2,1,0:T(4,128)S(1)} %get-tuple-element.10), channel_id=1, source_target_pairs={{0,1},{1,2},{2,3},{3,4},{4,5},{5,6},{6,7},{7,8},{8,9},{9,10},{10,1... | collective-permute-start | bytes 196616 | tf_op jit(solution)/shard_map/ppermute | solution.py:189
  8.1 6.5 %collective-permute-start.1 = (f32[32,4,128]{2,1,0:T(4,128)S(1)}, f32[32,4,128]{2,1,0:T(4,128)S(1)}, u32[]{:S(2)}, u32[]{:S(2)}) collective-permute-start(f32[32,4,128]{2,1,0:T(4,128)S(1)} %get-tuple-element.11), channel_id=1, source_target_pairs={{1,0},{2,1},{3,2},{4,3},{5,4},{6,5},{7,6},{8,7},{9,8},{10,9},{11,1... | collective-permute-start | bytes 196616 | tf_op jit(solution)/shard_map/ppermute | solution.py:190
  14.5 18.1 %copy-start.3 = (f32[32,128]{1,0:T(8,128)S(1)}, f32[32,128]{1,0:T(8,128)}, u32[]{:S(2)}) copy-start(f32[32,128]{1,0:T(8,128)} %coef_ref.3) | copy-start | bytes 49156
  14.5 18.1 %copy-start.4 = (f32[32,128]{1,0:T(8,128)S(1)}, f32[32,128]{1,0:T(8,128)}, u32[]{:S(2)}) copy-start(f32[32,128]{1,0:T(8,128)} %spacing_ref.1) | copy-start | bytes 49156
  14.6 16.3 %collective-permute-start.2 = (f32[424,128]{1,0:T(8,128)S(1)}, f32[424,128]{1,0:T(8,128)S(1)}, u32[]{:S(2)}, u32[]{:S(2)}) collective-permute-start(f32[424,128]{1,0:T(8,128)S(1)} %get-tuple-element.14), channel_id=1, source_target_pairs={{0,16},{16,32},{32,48},{48,64},{64,80},{80,96},{96,112},{112,128},... | collective-permute-start | bytes 651272 | tf_op jit(solution)/shard_map/ppermute | solution.py:192
  18.5 14.1 %collective-permute-start.3 = (f32[424,128]{1,0:T(8,128)S(1)}, f32[424,128]{1,0:T(8,128)S(1)}, u32[]{:S(2)}, u32[]{:S(2)}) collective-permute-start(f32[424,128]{1,0:T(8,128)S(1)} %get-tuple-element.15), channel_id=1, source_target_pairs={{16,0},{32,16},{48,32},{64,48},{80,64},{96,80},{112,96},{128,112},... | collective-permute-start | bytes 651272 | tf_op jit(solution)/shard_map/ppermute | solution.py:193

commit v2 on v0

v2 whole, which is shorter than its diff:
```python
import math

import jax
import jax.numpy as jnp
from jax import lax
from jax.experimental import pallas as pl
from jax.experimental.pallas import tpu as pltpu
from jax.sharding import PartitionSpec as P

SWEEPS = 4
HALO = 4
PLANES = 96
LAYER = 32
ROWS = 32
COLS = 128
WIDE = COLS + 2 * HALO
STEPS = WIDE // 8
STRIP_AT = WIDE - 7 * 8 - 1
STRIPS = HALO * PLANES
COEFS = STRIPS + 8 * HALO
MSG = COEFS + 8
F32 = jnp.float32
BF16 = jnp.bfloat16
COEF_AT = PLANES * ROWS
SPACING_AT = COEF_AT + ROWS
ALL = SPACING_AT + ROWS
VMEM = pl.BlockSpec(memory_space=pltpu.VMEM)


def nt(a, b):
    return lax.dot_general(a, b, (((1,), (1,)), ((), ())), preferred_element_type=F32)


def iota(shape, dim):
    return lax.broadcasted_iota(jnp.int32, shape, dim)


def call(kernel, ins, outs, scratch, cost, aliases=None):
    single = not isinstance(outs, (list, tuple))
    return pl.pallas_call(
        kernel,
        in_specs=[VMEM] * ins,
        out_shape=outs,
        out_specs=VMEM if single else [VMEM] * len(outs),
        scratch_shapes=scratch,
        input_output_aliases=aliases or {},
        compiler_params=pltpu.CompilerParams(vmem_limit_bytes=24 * 1024 * 1024),
        cost_estimate=pl.CostEstimate(flops=cost, bytes_accessed=2_000_000, transcendentals=0),
    )


def ring(line):
    return 17 * (line & 7) + (line >> 3)


def line_of(ref, r):
    return ref[pl.ds(pl.multiple_of(r * WIDE, 8), WIDE), :].reshape(STEPS, 8, COLS)


def put_line(ref, r, value):
    ref[pl.ds(pl.multiple_of(r * WIDE, 8), WIDE), :] = value.reshape(WIDE, COLS)


def put_plain(ref, r, value):
    for q in range(STEPS):
        ref[pl.ds(r * WIDE + q, 8, stride=STEPS), :] = value[q]


def put_strip(ref, r, strip):
    ref[pl.ds(r * WIDE + STRIP_AT, 8, stride=8), :] = strip


def opened(value, here, before):
    first = pltpu.roll(here[STEPS - 1], 1, 0)[None]
    last = pltpu.roll(here[0], 7, 0)[None]
    beside = jnp.concatenate([first, here[:-1]], axis=0) + jnp.concatenate([here[1:], last], axis=0)
    return (value - 4.0 * here) + (beside + before)


def selector():
    shape = (WIDE, COLS)
    return (ring(iota(shape, 0)) == iota(shape, 1)).astype(BF16)


def to_lanes(select, planes):
    pad = jnp.zeros((COLS - PLANES, COLS), BF16)
    return nt(select, jnp.concatenate([planes.astype(BF16), pad], axis=0))


def coef_strip(strip):
    return jnp.broadcast_to(strip[:, PLANES : PLANES + 1], (8, COLS))


def masked_ring(coef, scratch):
    rows = coef.shape[0]
    coef_t = jnp.transpose(jnp.concatenate([coef, jnp.zeros((COLS - rows, COLS), F32)], axis=0))
    place, last = lax.axis_index("normal"), lax.axis_size("normal") - 1
    col = iota((COLS, COLS), 0)
    outer = ((col == 0) & (place == 0)) | ((col == COLS - 1) & (place == last))
    scratch[pl.ds(0, COLS), :] = jnp.where(outer, 0.0, coef_t)
    scratch[pl.ds(COLS, 8), :] = jnp.zeros((8, COLS), F32)
    return jnp.concatenate([scratch[pl.ds(q, 8, stride=STEPS), :] for q in range(STEPS)], axis=0)


def line_sums(value, weight):
    high = value.astype(BF16)
    low = (value - high.astype(F32)).astype(BF16)
    both = lax.dot_general(
        jnp.concatenate([weight, weight], axis=1),
        jnp.concatenate([high, low], axis=0),
        (((1,), (0,)), ((), ())),
        preferred_element_type=F32,
    )
    return high, both[0:1] + both[2:3], both[1:2] + both[3:4]


def weight_of(weights, i):
    place = iota((16, COLS), 0)
    rows = [jnp.broadcast_to(weights[k * ROWS + i : k * ROWS + i + 1], (16, COLS)) for k in range(4)]
    rest = jnp.where(place == 2, rows[2], jnp.where(place == 3, rows[3], 0.0))
    return jnp.where(place == 0, rows[0], jnp.where(place == 1, rows[1], rest)).astype(BF16)


def split(value):
    high = value.astype(BF16).astype(F32)
    return high, value - high


def strip_kernel(all_ref, twin_ref, cross_ref, top_ref, bottom_ref):
    row, col = iota((2 * HALO, COLS), 0), iota((2 * HALO, COLS), 1)
    pick = (col == jnp.where(row < HALO, row, COLS - 2 * HALO + row)).astype(BF16)
    even = lax.axis_index("normal") % 2 == 0
    coef = all_ref[pl.ds(COEF_AT, ROWS), :]
    coef_t = jnp.transpose(jnp.concatenate([coef, jnp.zeros((COLS - ROWS, COLS), F32)], axis=0))
    ends = jnp.concatenate([coef_t[:HALO], coef_t[COLS - HALO :]], axis=0)
    pad = jnp.zeros((COLS - PLANES, COLS), BF16)
    for i in range(ROWS):
        planes = all_ref[pl.ds(i, PLANES, stride=ROWS), :]
        strip = nt(pick, jnp.concatenate([planes.astype(BF16), pad], axis=0))
        strip = jnp.where(col < PLANES, strip, jnp.broadcast_to(ends[:, i : i + 1], (2 * HALO, COLS)))
        twin_ref[i] = jnp.where(even, strip[HALO:], strip[:HALO])
        cross_ref[i] = jnp.where(even, strip[:HALO], strip[HALO:])
        if i < HALO:
            top_ref[pl.ds(i * PLANES, PLANES), :] = planes
        if i >= ROWS - HALO:
            bottom_ref[pl.ds((i - ROWS + HALO) * PLANES, PLANES), :] = planes
    zero = jnp.zeros((HALO, COLS), F32)
    top_ref[pl.ds(COEFS, 8), :] = jnp.concatenate([coef[:HALO], zero], axis=0)
    bottom_ref[pl.ds(COEFS, 8), :] = jnp.concatenate([coef[ROWS - HALO :], zero], axis=0)
    for ref in (top_ref, bottom_ref):
        ref[pl.ds(STRIPS, 8 * HALO), :] = jnp.zeros((8 * HALO, COLS), F32)


def corner_kernel(twin, cross, top_in, bottom_in, after_setup, top_ref, bottom_ref, strips_ref):
    even = lax.axis_index("normal") % 2 == 0
    right = jnp.where(even, twin[...], cross[...])
    left = jnp.where(even, cross[...], twin[...])
    strips = jnp.concatenate([right, left], axis=1)
    strips_ref[...] = strips
    top_ref[...] = top_in[...]
    bottom_ref[...] = bottom_in[...]
    for r in range(HALO):
        top_ref[pl.ds(STRIPS + 8 * r, 8), :] = strips[r]
        bottom_ref[pl.ds(STRIPS + 8 * r, 8), :] = strips[ROWS - HALO + r]


def setup_kernel(all_ref, v, f, weights, sums, ct):
    select = selector()
    ring_coef = masked_ring(all_ref[pl.ds(COEF_AT, ROWS), :], ct)
    for r in range(ROWS):
        v[pl.ds(r * WIDE, WIDE), :] = to_lanes(select, all_ref[pl.ds(r, PLANES, stride=ROWS), :])
        f[pl.ds(r * WIDE, WIDE), :] = jnp.broadcast_to(ring_coef[:, r : r + 1], (WIDE, COLS))
    spacing = all_ref[pl.ds(SPACING_AT, ROWS), :]
    earlier = (iota((COLS, COLS), 0) < iota((COLS, COLS), 1)).astype(F32)
    before = lax.dot_general(
        spacing, earlier, (((1,), (0,)), ((), ())), preferred_element_type=F32, precision=lax.Precision.HIGHEST
    )
    s_high, s_low = split(spacing)
    q_high, q_low = split(before * spacing)
    weights[...] = jnp.concatenate([s_high, q_high, s_low, q_low], axis=0)
    total = jnp.broadcast_to(jnp.sum(spacing, axis=1, keepdims=True), (ROWS, COLS))
    empty = jnp.zeros((ROWS, COLS), F32)
    sums[...] = jnp.concatenate([empty, empty, total, empty], axis=0)


def inner_kernel(v_in, f_in, strips, weights, sums_in, v, f, kept, part, sums):
    for r in range(ROWS):
        put_strip(v, r, strips[r])
        put_strip(f, r, coef_strip(strips[r]))

    for sweep in range(SWEEPS):
        put = put_line if sweep < SWEEPS - 1 else put_plain
        low, high = sweep + 1, ROWS - 2 - sweep

        def step(r, held):
            sofar, here = held
            value = line_of(v, r + 1)
            after = line_of(f, r + 1) * value
            put(v, r, sofar + after)
            return opened(value, after, here), after

        value = line_of(v, low)
        here = line_of(f, low) * value
        put_line(kept, sweep, here)
        held = (opened(value, here, line_of(f, low - 1) * line_of(v, low - 1)), here)
        held = lax.fori_loop(low, high, step, held, unroll=4)
        put_line(kept, HALO + sweep, held[1])
        put(v, high, held[0] + line_of(f, high + 1) * line_of(v, high + 1))

    sums[...] = sums_in[...]
    eye = (iota((PLANES, COLS), 0) == iota((PLANES, COLS), 1)).astype(BF16)
    for i in range(HALO, ROWS - HALO):
        high, p, q = line_sums(v[pl.ds(i * WIDE, COLS), :], weight_of(weights[...], i))
        sums[pl.ds(i, 1), :] = p
        sums[pl.ds(ROWS + i, 1), :] = q
        part[pl.ds(i, PLANES, stride=ROWS), :] = nt(eye, high)


def outer_kernel(above, below, v, f, kept, part, sums_in, weights, out_ref, send_ref, hv, hf, hw, ct, xe, plain, sums):
    select = selector()
    ring_coef = masked_ring(jnp.concatenate([above[pl.ds(COEFS, HALO), :], below[pl.ds(COEFS, HALO), :]], axis=0), ct)
    for k in range(HALO):
        for message, at, c in ((above, k, k), (below, 3 * HALO + k, HALO + k)):
            hv[pl.ds(at * WIDE, WIDE), :] = to_lanes(select, message[pl.ds(k * PLANES, PLANES), :])
            hf[pl.ds(at * WIDE, WIDE), :] = jnp.broadcast_to(ring_coef[:, c : c + 1], (WIDE, COLS))
            strip = message[pl.ds(STRIPS + 8 * k, 8), :]
            put_strip(hv, at, strip)
            put_strip(hf, at, coef_strip(strip))
    own = {HALO + k: k for k in range(HALO)} | {2 * HALO + k: ROWS - HALO + k for k in range(HALO)}
    moved = set()

    def value_of(e):
        return line_of(v, own[e]) if e in own and e not in moved else line_of(hv, e)

    def coef_of(e):
        return line_of(f, own[e]) if e in own else line_of(hf, e)

    def chain(first, before, last_after):
        value = value_of(first)
        here = coef_of(first) * value
        sofar = opened(value, here, before)
        for e in range(first, first + HALO):
            if e == first + HALO - 1 and last_after is not None:
                put_line(hv, e, sofar + last_after)
            else:
                value = value_of(e + 1)
                after = coef_of(e + 1) * value
                put_line(hv, e, sofar + after)
                if e < first + HALO - 1:
                    sofar = opened(value, after, here)
                here = after
            moved.add(e)

    for sweep in range(SWEEPS):
        chain(sweep + 1, coef_of(sweep) * value_of(sweep), line_of(kept, sweep))
        chain(3 * HALO - 1 - sweep, line_of(kept, HALO + sweep), None)
    sums[...] = sums_in[...]
    eye = (iota((PLANES, COLS), 0) == iota((PLANES, COLS), 1)).astype(BF16)
    for k in range(2 * HALO):
        i = k if k < HALO else ROWS - 2 * HALO + k
        put_plain(plain, k, line_of(hv, HALO + k))
        high, p, q = line_sums(plain[pl.ds(k * WIDE, COLS), :], weight_of(weights[...], i))
        sums[pl.ds(i, 1), :] = p
        sums[pl.ds(ROWS + i, 1), :] = q
        xe[pl.ds(k, PLANES, stride=2 * HALO), :] = nt(eye, high)
    tiles = part[...].reshape(PLANES, ROWS // 8, 8, COLS)
    ends = xe[...].reshape(PLANES, 8, COLS)
    near = iota((PLANES, 8, COLS), 1) < HALO
    head = jnp.where(near, ends, tiles[:, 0])
    tail = jnp.where(near, tiles[:, 3], ends)
    out_ref[...] = jnp.concatenate([head, tiles[:, 1], tiles[:, 2], tail], axis=1).astype(BF16)
    sums[...] = jnp.transpose(sums[...])
    owners = send_ref.shape[0]
    each = LAYER // owners
    for c in range(3):
        for e in range(each):
            send_ref[:, c * each + e, :] = sums[pl.ds(c * LAYER + e, owners, stride=each), :]
    send_ref[:, 3 * each :, :] = jnp.zeros((owners, 8 - 3 * each, COLS), F32)


def owner_kernel(got_ref, out_ref):
    owners = got_ref.shape[0]
    each = LAYER // owners
    own = [pltpu.roll(got_ref[d], COLS - 2 * ROWS, 1) for d in range(owners)]
    total = own[0]
    for d in range(1, owners):
        total = total + own[d]
    rest = total
    acc = jnp.zeros_like(total)
    moment = jnp.zeros_like(total)
    for d in range(owners):
        acc = acc + got_ref[d] * rest
        moment = moment + got_ref[d]
        rest = rest - own[d]
    acc = acc - pltpu.roll(moment, COLS - ROWS, 1)
    value = (acc / total) / total * math.sqrt(COLS * owners)
    for c in range(3):
        out_ref[c] = value[c * each : (c + 1) * each, :ROWS]


def shaped(*shape):
    return jax.ShapeDtypeStruct(shape, F32)


def lines(count):
    return pltpu.VMEM((count * WIDE, COLS), F32)


def body(adjoint_in, coef, spacing):
    wraps, owners = lax.axis_size("wrap"), lax.axis_size("normal")
    everything = jnp.concatenate([adjoint_in.reshape(PLANES * ROWS, COLS).astype(F32), coef, spacing], axis=0)
    strip, message, square = shaped(ROWS, HALO, COLS), shaped(MSG, COLS), shaped(COLS, COLS)
    own_rows = shaped(ROWS * WIDE, COLS)
    twin, cross, top, bottom = call(strip_kernel, 1, [strip, strip, message, message], [], 10_000_000)(everything)
    cross = lax.ppermute(cross, "normal", [(k, k + 1 if k % 2 else k - 1) for k in range(1, owners - 1)])
    twin = lax.ppermute(twin, "normal", [(k, k ^ 1) for k in range(owners)])
    v, f, weights, sums = call(
        setup_kernel, 1, [own_rows, own_rows, square, square], [pltpu.VMEM((WIDE, COLS), F32)], 20_000_000
    )(everything)
    top, bottom, strips = call(corner_kernel, 5, [message, message, shaped(ROWS, 8, COLS)], [], 1_000_000)(
        twin, cross, top, bottom, sums
    )
    above = lax.ppermute(bottom, "wrap", [(k, (k + 1) % wraps) for k in range(wraps)])
    below = lax.ppermute(top, "wrap", [((k + 1) % wraps, k) for k in range(wraps)])
    v, f, kept, part, sums = call(
        inner_kernel,
        5,
        [own_rows, own_rows, shaped(2 * HALO * WIDE, COLS), shaped(PLANES * ROWS, COLS), square],
        [],
        50_000_000,
        {0: 0, 1: 1},
    )(v, f, strips, weights, sums)
    adjoint_out, sums = call(
        outer_kernel,
        8,
        [jax.ShapeDtypeStruct((PLANES, ROWS, COLS), BF16), shaped(owners, 8, COLS)],
        [
            lines(4 * HALO),
            lines(4 * HALO),
            lines(1),
            pltpu.VMEM((WIDE, COLS), F32),
            pltpu.VMEM((PLANES * 2 * HALO, COLS), F32),
            lines(2 * HALO),
            pltpu.VMEM((COLS, COLS), F32),
        ],
        10_000_000,
    )(above, below, v, f, kept, part, sums, weights)
    got = lax.all_to_all(sums, "normal", 0, 0, tiled=True)
    wall_sens = call(owner_kernel, 1, shaped(3, LAYER // owners, ROWS), [], 100_000)(got)
    return adjoint_out.reshape(3, LAYER, ROWS, COLS), wall_sens


def solution(mesh):
    placed = (P(None, None, "wrap", "normal"), P("wrap", "normal"), P("wrap", "normal"))
    return jax.shard_map(
        body,
        mesh=mesh,
        in_specs=placed,
        out_specs=(P(None, None, "wrap", "normal"), P(None, "normal", "wrap")),
        check_vma=False,
    )
```

time: 221 us -> 46.4 us (0.21)
  the two profiles are of different devices: /device:TPU:8 before, /device:TPU:1 now
where the time goes in v2:
time: 46.4 us; the launch traced here: 46.2 us
  starting transfers between devices  21 us (45%)
  blocking collectives  11.8 us (25%)
  Pallas kernels  8.77 us (19%)
  waiting for transfers between devices  2.51 us (5%)
  other arithmetic  1.35 us (3%)
  between operations  0.74 us (2%)
    all_to_all x1, blocking collectives, body(): got = lax.all_to_all(sums, 'normal', 0, 0, tiled=True)  11.8 us
    ppermute x1, starting transfers between devices, body(): twin = lax.ppermute(twin, 'normal', [(k, k ^ 1) for k in range(owners)])  8.78 us
    ppermute x1, starting transfers between devices, body(): lax.ppermute(top, 'wrap', [((k + 1) % wraps, k) for k in range(wraps)])  8.38 us
    pallas_call x1, Pallas kernels, body(): call(inner_kernel, 5, [own_rows, own_rows, shaped(2 * HALO * WIDE, COLS),...  3.43 us
    ppermute x1, waiting for transfers between devices, body(): lax.ppermute(cross, 'normal', [(k, k + 1 if k % 2 else k - 1) for k in ra...  2.15 us
    pallas_call x1, Pallas kernels, body(): call(outer_kernel, 8, [jax.ShapeDtypeStruct((PLANES, ROWS, COLS), BF16),...  2.14 us
    ppermute x1, starting transfers between devices, body(): lax.ppermute(cross, 'normal', [(k, k + 1 if k % 2 else k - 1) for k in ra...  1.92 us
    ppermute x1, starting transfers between devices, body(): lax.ppermute(bottom, 'wrap', [(k, (k + 1) % wraps) for k in range(wraps)])  1.92 us
  transfers between devices with their start and end apart: 4, of which 2 were waited for; matrix products, arithmetic and copies ran while one was open for 0% of the time, Pallas kernels for 11%

profile of v2, /device:TPU:1, one launch (start us, length us, event | category | flops | bytes accessed | tf_op | source)
XLA Modules:
  0.0 46.2 jit_solution(28166612253801326)
XLA Ops:
  0.6 0.0 copy-start
  0.6 0.0 copy-start.1
  0.6 1.2 %bitcast_convert_fusion = f32[3072,128]{1,0:T(8,128)S(1)} fusion(bf16[3,32,32,128]{3,2,1,0:T(8,128)(2,1)} %param.3), kind=kLoop, calls=%fused_computation.1 | loop fusion | flops 393216 | bytes 2359296 | tf_op jit(solution)/shard_map/convert_element_type | solution.py:311
  1.9 0.0 copy-done
  1.9 0.0 copy-done.1
  1.9 0.1 pad_maximum_fusion.all_ref
  2.0 1.0 %shard_map.50 = (f32[32,4,128]{2,1,0:T(4,128)S(1)}, f32[32,4,128]{2,1,0:T(4,128)S(1)}, f32[424,128]{1,0:T(8,128)S(1)}, f32[424,128]{1,0:T(8,128)S(1)}) custom-call(f32[3136,128]{1,0:T(8,128)S(1)} %pad_maximum_fusion.all_ref), custom_call_target="tpu_custom_call" | custom-call | flops 10000000 | bytes 2000000 | tf_op jit(solution)/shard_map/pallas_call | solution.py:314
  3.0 8.8 %collective-permute-start = (f32[32,4,128]{2,1,0:T(4,128)S(1)}, f32[32,4,128]{2,1,0:T(4,128)S(1)}, u32[]{:S(2)}, u32[]{:S(2)}) collective-permute-start(f32[32,4,128]{2,1,0:T(4,128)S(1)} %get-tuple-element.20), channel_id=1, source_target_pairs={{0,1},{1,0},{2,3},{3,2},{4,5},{5,4},{6,7},{7,6},{8,9},{9,8},{10,11... | collective-permute-start | bytes 196616 | tf_op jit(solution)/shard_map/ppermute | solution.py:316
  11.8 1.9 %collective-permute-start.1 = (f32[32,4,128]{2,1,0:T(4,128)S(1)}, f32[32,4,128]{2,1,0:T(4,128)S(1)}, u32[]{:S(2)}, u32[]{:S(2)}) collective-permute-start(f32[32,4,128]{2,1,0:T(4,128)S(1)} %get-tuple-element.21), channel_id=1, source_target_pairs={{1,2},{2,1},{3,4},{4,3},{5,6},{6,5},{7,8},{8,7},{9,10},{10,9},{11,... | collective-permute-start | bytes 196616 | tf_op jit(solution)/shard_map/ppermute | solution.py:315
  13.7 1.5 %shard_map.51 = (f32[4352,128]{1,0:T(8,128)S(1)}, f32[4352,128]{1,0:T(8,128)S(1)}, f32[128,128]{1,0:T(8,128)S(1)}, f32[128,128]{1,0:T(8,128)S(1)}) custom-call(f32[3136,128]{1,0:T(8,128)S(1)} %pad_maximum_fusion.all_ref), custom_call_target="tpu_custom_call" | custom-call | flops 20000000 | bytes 2000000 | tf_op jit(solution)/shard_map/pallas_call | solution.py:317
  15.2 0.0 collective-permute-done.twin
  15.2 2.2 %collective-permute-done.1.cross = f32[32,4,128]{2,1,0:T(4,128)S(1)} collective-permute-done((f32[32,4,128]{2,1,0:T(4,128)S(1)}, f32[32,4,128]{2,1,0:T(4,128)S(1)}, u32[]{:S(2)}, u32[]{:S(2)}) %collective-permute-start.1) | collective-permute-done | bytes 65568 | tf_op jit(solution)/shard_map/ppermute | solution.py:315
  17.4 0.1 shard_map.52
  17.4 1.9 %collective-permute-start.2 = (f32[424,128]{1,0:T(8,128)S(1)}, f32[424,128]{1,0:T(8,128)S(1)}, u32[]{:S(2)}, u32[]{:S(2)}) collective-permute-start(f32[424,128]{1,0:T(8,128)S(1)} %get-tuple-element.25), channel_id=1, source_target_pairs={{0,16},{16,32},{32,48},{48,64},{64,80},{80,96},{96,112},{112,128},... | collective-permute-start | bytes 651272 | tf_op jit(solution)/shard_map/ppermute | solution.py:323
  19.4 8.4 %collective-permute-start.3 = (f32[424,128]{1,0:T(8,128)S(1)}, f32[424,128]{1,0:T(8,128)S(1)}, u32[]{:S(2)}, u32[]{:S(2)}) collective-permute-start(f32[424,128]{1,0:T(8,128)S(1)} %get-tuple-element.26), channel_id=1, source_target_pairs={{16,0},{32,16},{48,32},{64,48},{80,64},{96,80},{112,96},{128,112},... | collective-permute-start | bytes 651272 | tf_op jit(solution)/shard_map/ppermute | solution.py:324
  27.8 3.4 %shard_map.53 = (f32[4352,128]{1,0:T(8,128)S(1)}, f32[4352,128]{1,0:T(8,128)S(1)}, f32[1088,128]{1,0:T(8,128)S(1)}, f32[3072,128]{1,0:T(8,128)S(1)}, f32[128,128]{1,0:T(8,128)S(1)}) custom-call(f32[4352,128]{1,0:T(8,128)S(1)} %get-tuple-element.27.v_in, f32[4352,128]{1,0:T(8,128)S(1)} %get-tuple-element.28.f_in, ...), custom_call_target="tpu_custom_call", output_to_operand_aliasing={{0}: (0, {}), {1}: (1, {})} | custom-call | flops 50000000 | bytes 2000000 | tf_op jit(solution)/shard_map/pallas_call | solution.py:325
  31.2 0.0 collective-permute-done.2.above
  31.2 0.4 collective-permute-done.3.below
  31.6 2.1 %shard_map.54 = (bf16[96,32,128]{2,1,0:T(8,128)(2,1)}, f32[16,8,128]{2,1,0:T(8,128)S(1)}) custom-call(f32[424,128]{1,0:T(8,128)S(1)} %collective-permute-done.2.above, f32[424,128]{1,0:T(8,128)S(1)} %collective-permute-done.3.below, f32[4352,128]{1,0:T(8,128)S(1)} %get-tuple-element.31.v, f32[4352,128]{1,0:T(8,128)S(1)} %get-tuple-element.32.f, ...), custom_call_target="tpu_custom_call" | custom-call | flops 10000000 | bytes 2000000 | tf_op jit(solution)/shard_map/pallas_call | solution.py:333
  33.7 11.8 %all_to_all.5.got_ref = f32[16,8,128]{2,1,0:T(8,128)S(1)} all-to-all(f32[16,8,128]{2,1,0:T(8,128)S(1)} %get-tuple-element.37), channel_id=1, replica_groups=mesh['wrap'=32,'normal'=16] {'normal'}, dimensions={0} | all-to-all | bytes 131072 | tf_op jit(solution)/shard_map/all_to_all | solution.py:348
  45.5 0.7 %shard_map.55 = f32[3,2,32]{2,1,0:T(2,128)} custom-call(f32[16,8,128]{2,1,0:T(8,128)S(1)} %all_to_all.5.got_ref), custom_call_target="tpu_custom_call" | custom-call | flops 100000 | bytes 2000000 | tf_op jit(solution)/shard_map/pallas_call | solution.py:349
Async XLA Ops:
  0.6 1.3 %copy-start = (f32[32,128]{1,0:T(8,128)S(1)}, f32[32,128]{1,0:T(8,128)}, u32[]{:S(2)}) copy-start(f32[32,128]{1,0:T(8,128)} %param.5) | copy-start | bytes 49156
  0.6 1.3 %copy-start.1 = (f32[32,128]{1,0:T(8,128)S(1)}, f32[32,128]{1,0:T(8,128)}, u32[]{:S(2)}) copy-start(f32[32,128]{1,0:T(8,128)} %param.4) | copy-start | bytes 49156
  3.0 12.2 %collective-permute-start = (f32[32,4,128]{2,1,0:T(4,128)S(1)}, f32[32,4,128]{2,1,0:T(4,128)S(1)}, u32[]{:S(2)}, u32[]{:S(2)}) collective-permute-start(f32[32,4,128]{2,1,0:T(4,128)S(1)} %get-tuple-element.20), channel_id=1, source_target_pairs={{0,1},{1,0},{2,3},{3,2},{4,5},{5,4},{6,7},{7,6},{8,9},{9,8},{10,11... | collective-permute-start | bytes 196616 | tf_op jit(solution)/shard_map/ppermute | solution.py:316
  11.8 5.6 %collective-permute-start.1 = (f32[32,4,128]{2,1,0:T(4,128)S(1)}, f32[32,4,128]{2,1,0:T(4,128)S(1)}, u32[]{:S(2)}, u32[]{:S(2)}) collective-permute-start(f32[32,4,128]{2,1,0:T(4,128)S(1)} %get-tuple-element.21), channel_id=1, source_target_pairs={{1,2},{2,1},{3,4},{4,3},{5,6},{6,5},{7,8},{8,7},{9,10},{10,9},{11,... | collective-permute-start | bytes 196616 | tf_op jit(solution)/shard_map/ppermute | solution.py:315
  17.4 13.8 %collective-permute-start.2 = (f32[424,128]{1,0:T(8,128)S(1)}, f32[424,128]{1,0:T(8,128)S(1)}, u32[]{:S(2)}, u32[]{:S(2)}) collective-permute-start(f32[424,128]{1,0:T(8,128)S(1)} %get-tuple-element.25), channel_id=1, source_target_pairs={{0,16},{16,32},{32,48},{48,64},{64,80},{80,96},{96,112},{112,128},... | collective-permute-start | bytes 651272 | tf_op jit(solution)/shard_map/ppermute | solution.py:323
  19.4 12.2 %collective-permute-start.3 = (f32[424,128]{1,0:T(8,128)S(1)}, f32[424,128]{1,0:T(8,128)S(1)}, u32[]{:S(2)}, u32[]{:S(2)}) collective-permute-start(f32[424,128]{1,0:T(8,128)S(1)} %get-tuple-element.26), channel_id=1, source_target_pairs={{16,0},{32,16},{48,32},{64,48},{80,64},{96,80},{112,96},{128,112},... | collective-permute-start | bytes 651272 | tf_op jit(solution)/shard_map/ppermute | solution.py:324

commit v3 on v2

--- a/solution.py
+++ b/solution.py
@@ -16,9 +16,9 @@
 WIDE = COLS + 2 * HALO
 STEPS = WIDE // 8
 STRIP_AT = WIDE - 7 * 8 - 1
-STRIPS = HALO * PLANES
-COEFS = STRIPS + 8 * HALO
-MSG = COEFS + 8
+COEFS = HALO * PLANES
+MAIN = COEFS + 8
+MSG = MAIN + 8 * HALO
 F32 = jnp.float32
 BF16 = jnp.bfloat16
 COEF_AT = PLANES * ROWS
@@ -45,7 +45,7 @@
         scratch_shapes=scratch,
         input_output_aliases=aliases or {},
         compiler_params=pltpu.CompilerParams(vmem_limit_bytes=24 * 1024 * 1024),
-        cost_estimate=pl.CostEstimate(flops=cost, bytes_accessed=2_000_000, transcendentals=0),
+        cost_estimate=pl.CostEstimate(flops=cost, bytes_accessed=1_000, transcendentals=0),
     )
 
 
@@ -126,7 +126,15 @@
     return high, value - high
 
 
-def strip_kernel(all_ref, twin_ref, cross_ref, top_ref, bottom_ref):
+def rows_kernel(all_ref, after_setup, top_ref, bottom_ref):
+    zero = jnp.zeros((HALO, COLS), F32)
+    for ref, at in ((top_ref, 0), (bottom_ref, ROWS - HALO)):
+        for k in range(HALO):
+            ref[pl.ds(k * PLANES, PLANES), :] = all_ref[pl.ds(at + k, PLANES, stride=ROWS), :]
+        ref[pl.ds(COEFS, 8), :] = jnp.concatenate([all_ref[pl.ds(COEF_AT + at, HALO), :], zero], axis=0)
+
+
+def strip_kernel(all_ref, cross_ref, twin_ref):
     row, col = iota((2 * HALO, COLS), 0), iota((2 * HALO, COLS), 1)
     pick = (col == jnp.where(row < HALO, row, COLS - 2 * HALO + row)).astype(BF16)
     even = lax.axis_index("normal") % 2 == 0
@@ -138,33 +146,28 @@
         planes = all_ref[pl.ds(i, PLANES, stride=ROWS), :]
         strip = nt(pick, jnp.concatenate([planes.astype(BF16), pad], axis=0))
         strip = jnp.where(col < PLANES, strip, jnp.broadcast_to(ends[:, i : i + 1], (2 * HALO, COLS)))
+        cross_ref[i] = jnp.where(even, strip[:HALO], strip[HALO:])
         twin_ref[i] = jnp.where(even, strip[HALO:], strip[:HALO])
-        cross_ref[i] = jnp.where(even, strip[:HALO], strip[HALO:])
-        if i < HALO:
-            top_ref[pl.ds(i * PLANES, PLANES), :] = planes
-        if i >= ROWS - HALO:
-            bottom_ref[pl.ds((i - ROWS + HALO) * PLANES, PLANES), :] = planes
-    zero = jnp.zeros((HALO, COLS), F32)
-    top_ref[pl.ds(COEFS, 8), :] = jnp.concatenate([coef[:HALO], zero], axis=0)
-    bottom_ref[pl.ds(COEFS, 8), :] = jnp.concatenate([coef[ROWS - HALO :], zero], axis=0)
-    for ref in (top_ref, bottom_ref):
-        ref[pl.ds(STRIPS, 8 * HALO), :] = jnp.zeros((8 * HALO, COLS), F32)
-
-
-def corner_kernel(twin, cross, top_in, bottom_in, after_setup, top_ref, bottom_ref, strips_ref):
+
+
+def pass_kernel(ref, out_ref):
+    out_ref[...] = ref[...]
+
+
+def corner_kernel(cross, twin, top, bottom, strips_ref, top_ref, bottom_ref):
     even = lax.axis_index("normal") % 2 == 0
     right = jnp.where(even, twin[...], cross[...])
     left = jnp.where(even, cross[...], twin[...])
     strips = jnp.concatenate([right, left], axis=1)
     strips_ref[...] = strips
-    top_ref[...] = top_in[...]
-    bottom_ref[...] = bottom_in[...]
+    top_ref[pl.ds(0, MAIN), :] = top[...]
+    bottom_ref[pl.ds(0, MAIN), :] = bottom[...]
     for r in range(HALO):
-        top_ref[pl.ds(STRIPS + 8 * r, 8), :] = strips[r]
-        bottom_ref[pl.ds(STRIPS + 8 * r, 8), :] = strips[ROWS - HALO + r]
-
-
-def setup_kernel(all_ref, v, f, weights, sums, ct):
+        top_ref[pl.ds(MAIN + 8 * r, 8), :] = strips[r]
+        bottom_ref[pl.ds(MAIN + 8 * r, 8), :] = strips[ROWS - HALO + r]
+
+
+def setup_kernel(all_ref, after_strip, v, f, weights, sums, ct):
     select = selector()
     ring_coef = masked_ring(all_ref[pl.ds(COEF_AT, ROWS), :], ct)
     for r in range(ROWS):
@@ -216,14 +219,14 @@
         part[pl.ds(i, PLANES, stride=ROWS), :] = nt(eye, high)
 
 
-def outer_kernel(above, below, v, f, kept, part, sums_in, weights, out_ref, send_ref, hv, hf, hw, ct, xe, plain, sums):
+def outer_kernel(above, below, v, f, kept, sums_in, weights, xe, send_ref, hv, hf, ct, plain, sums):
     select = selector()
     ring_coef = masked_ring(jnp.concatenate([above[pl.ds(COEFS, HALO), :], below[pl.ds(COEFS, HALO), :]], axis=0), ct)
     for k in range(HALO):
         for message, at, c in ((above, k, k), (below, 3 * HALO + k, HALO + k)):
             hv[pl.ds(at * WIDE, WIDE), :] = to_lanes(select, message[pl.ds(k * PLANES, PLANES), :])
             hf[pl.ds(at * WIDE, WIDE), :] = jnp.broadcast_to(ring_coef[:, c : c + 1], (WIDE, COLS))
-            strip = message[pl.ds(STRIPS + 8 * k, 8), :]
+            strip = message[pl.ds(MAIN + 8 * k, 8), :]
             put_strip(hv, at, strip)
             put_strip(hf, at, coef_strip(strip))
     own = {HALO + k: k for k in range(HALO)} | {2 * HALO + k: ROWS - HALO + k for k in range(HALO)}
@@ -263,12 +266,6 @@
         sums[pl.ds(i, 1), :] = p
         sums[pl.ds(ROWS + i, 1), :] = q
         xe[pl.ds(k, PLANES, stride=2 * HALO), :] = nt(eye, high)
-    tiles = part[...].reshape(PLANES, ROWS // 8, 8, COLS)
-    ends = xe[...].reshape(PLANES, 8, COLS)
-    near = iota((PLANES, 8, COLS), 1) < HALO
-    head = jnp.where(near, ends, tiles[:, 0])
-    tail = jnp.where(near, tiles[:, 3], ends)
-    out_ref[...] = jnp.concatenate([head, tiles[:, 1], tiles[:, 2], tail], axis=1).astype(BF16)
     sums[...] = jnp.transpose(sums[...])
     owners = send_ref.shape[0]
     each = LAYER // owners
@@ -278,7 +275,13 @@
     send_ref[:, 3 * each :, :] = jnp.zeros((owners, 8 - 3 * each, COLS), F32)
 
 
-def owner_kernel(got_ref, out_ref):
+def final_kernel(got_ref, part, xe, out_ref, wall_ref):
+    tiles = part[...].reshape(PLANES, ROWS // 8, 8, COLS)
+    ends = xe[...].reshape(PLANES, 8, COLS)
+    near = iota((PLANES, 8, COLS), 1) < HALO
+    head = jnp.where(near, ends, tiles[:, 0])
+    tail = jnp.where(near, tiles[:, 3], ends)
+    out_ref[...] = jnp.concatenate([head, tiles[:, 1], tiles[:, 2], tail], axis=1).astype(BF16)
     owners = got_ref.shape[0]
     each = LAYER // owners
     own = [pltpu.roll(got_ref[d], COLS - 2 * ROWS, 1) for d in range(owners)]
@@ -295,7 +298,7 @@
     acc = acc - pltpu.roll(moment, COLS - ROWS, 1)
     value = (acc / total) / total * math.sqrt(COLS * owners)
     for c in range(3):
-        out_ref[c] = value[c * each : (c + 1) * each, :ROWS]
+        wall_ref[c] = value[c * each : (c + 1) * each, :ROWS]
 
 
 def shaped(*shape):
@@ -309,16 +312,19 @@
 def body(adjoint_in, coef, spacing):
     wraps, owners = lax.axis_size("wrap"), lax.axis_size("normal")
     everything = jnp.concatenate([adjoint_in.reshape(PLANES * ROWS, COLS).astype(F32), coef, spacing], axis=0)
-    strip, message, square = shaped(ROWS, HALO, COLS), shaped(MSG, COLS), shaped(COLS, COLS)
+    strip, square = shaped(ROWS, HALO, COLS), shaped(COLS, COLS)
     own_rows = shaped(ROWS * WIDE, COLS)
-    twin, cross, top, bottom = call(strip_kernel, 1, [strip, strip, message, message], [], 10_000_000)(everything)
-    cross = lax.ppermute(cross, "normal", [(k, k + 1 if k % 2 else k - 1) for k in range(1, owners - 1)])
-    twin = lax.ppermute(twin, "normal", [(k, k ^ 1) for k in range(owners)])
+    to_cross, to_twin = call(strip_kernel, 1, [strip, strip], [], 1_000)(everything)
+    to_twin = call(pass_kernel, 1, strip, [], 1_000)(to_twin)
+    cross = lax.ppermute(to_cross, "normal", [(k, k + 1 if k % 2 else k - 1) for k in range(1, owners - 1)])
+    cross = call(pass_kernel, 1, strip, [], 1_000)(cross)
+    twin = lax.ppermute(to_twin, "normal", [(k, k ^ 1) for k in range(owners)])
     v, f, weights, sums = call(
-        setup_kernel, 1, [own_rows, own_rows, square, square], [pltpu.VMEM((WIDE, COLS), F32)], 20_000_000
-    )(everything)
-    top, bottom, strips = call(corner_kernel, 5, [message, message, shaped(ROWS, 8, COLS)], [], 1_000_000)(
-        twin, cross, top, bottom, sums
+        setup_kernel, 2, [own_rows, own_rows, square, square], [pltpu.VMEM((WIDE, COLS), F32)], 1_000
+    )(everything, to_twin)
+    top, bottom = call(rows_kernel, 2, [shaped(MAIN, COLS)] * 2, [], 1_000)(everything, sums)
+    strips, top, bottom = call(corner_kernel, 4, [shaped(ROWS, 8, COLS), shaped(MSG, COLS), shaped(MSG, COLS)], [], 1_000)(
+        cross, twin, top, bottom
     )
     above = lax.ppermute(bottom, "wrap", [(k, (k + 1) % wraps) for k in range(wraps)])
     below = lax.ppermute(top, "wrap", [((k + 1) % wraps, k) for k in range(wraps)])
@@ -327,26 +333,24 @@
         5,
         [own_rows, own_rows, shaped(2 * HALO * WIDE, COLS), shaped(PLANES * ROWS, COLS), square],
         [],
-        50_000_000,
+        20_000_000_000,
         {0: 0, 1: 1},
     )(v, f, strips, weights, sums)
-    adjoint_out, sums = call(
+    ends, sums = call(
         outer_kernel,
-        8,
-        [jax.ShapeDtypeStruct((PLANES, ROWS, COLS), BF16), shaped(owners, 8, COLS)],
-        [
-            lines(4 * HALO),
-            lines(4 * HALO),
-            lines(1),
-            pltpu.VMEM((WIDE, COLS), F32),
-            pltpu.VMEM((PLANES * 2 * HALO, COLS), F32),
-            lines(2 * HALO),
-            pltpu.VMEM((COLS, COLS), F32),
-        ],
-        10_000_000,
-    )(above, below, v, f, kept, part, sums, weights)
+        7,
+        [shaped(PLANES * 2 * HALO, COLS), shaped(owners, 8, COLS)],
+        [lines(4 * HALO), lines(4 * HALO), pltpu.VMEM((WIDE, COLS), F32), lines(2 * HALO), pltpu.VMEM((COLS, COLS), F32)],
+        1_000,
+    )(above, below, v, f, kept, sums, weights)
     got = lax.all_to_all(sums, "normal", 0, 0, tiled=True)
-    wall_sens = call(owner_kernel, 1, shaped(3, LAYER // owners, ROWS), [], 100_000)(got)
+    adjoint_out, wall_sens = call(
+        final_kernel,
+        3,
+        [jax.ShapeDtypeStruct((PLANES, ROWS, COLS), BF16), shaped(3, LAYER // owners, ROWS)],
+        [],
+        1_000,
+    )(got, part, ends)
     return adjoint_out.reshape(3, LAYER, ROWS, COLS), wall_sens
 
 

time: 46.4 us -> 45.3 us (0.976)
  waiting for transfers between devices: 2.51 us -> 0.81 us
  starting transfers between devices: 21 us -> 22.1 us
  blocking collectives: 11.8 us -> 11.2 us
    ppermute x1, starting transfers between devices: 8.38 us -> 10.7 us  [body(): lax.ppermute(top, 'wrap', [((k + 1) % wraps, k) for k in range(wraps)])]
    ppermute x2, waiting for transfers between devices: 2.15 us -> 0.01 us  [the longest x1 0.01 us: body(): lax.ppermute(to_cross, 'normal', [(k, k + 1 if k % 2 else k - 1) for k in...]
    ppermute x2, starting transfers between devices: 10.7 us -> 9.44 us  [the longest x1 4.94 us: body(): twin = lax.ppermute(to_twin, 'normal', [(k, k ^ 1) for k in range(owners)])]
    all_to_all x1, blocking collectives: 11.8 us -> 11.2 us  [body(): got = lax.all_to_all(sums, 'normal', 0, 0, tiled=True)]
    pallas_call x5 -> x8, Pallas kernels: 5.34 us -> 5.25 us  [the longest x1 1.49 us: body(): call(setup_kernel, 2, [own_rows, own_rows, square, square], [pltpu.VMEM((...]
  transfers between devices with their start and end apart: 4 -> 4, of which waited for: 2 -> 1; matrix products, arithmetic and copies ran while one was open for 0% -> 0% of each run, Pallas kernels for 11% -> 12%
where the time goes in v3:
time: 45.3 us; the launch traced here: 45 us
  starting transfers between devices  22.1 us (49%)
  blocking collectives  11.2 us (25%)
  Pallas kernels  8.68 us (19%)
  other arithmetic  1.35 us (3%)
  waiting for transfers between devices  0.81 us (2%)
  between operations  0.78 us (2%)
    all_to_all x1, blocking collectives, body(): got = lax.all_to_all(sums, 'normal', 0, 0, tiled=True)  11.2 us
    ppermute x1, starting transfers between devices, body(): lax.ppermute(top, 'wrap', [((k + 1) % wraps, k) for k in range(wraps)])  10.7 us
    ppermute x1, starting transfers between devices, body(): twin = lax.ppermute(to_twin, 'normal', [(k, k ^ 1) for k in range(owners)])  4.94 us
    ppermute x1, starting transfers between devices, body(): lax.ppermute(to_cross, 'normal', [(k, k + 1 if k % 2 else k - 1) for k in...  4.5 us
    pallas_call x1, Pallas kernels, body(): call(inner_kernel, 5, [own_rows, own_rows, shaped(2 * HALO * WIDE, COLS),...  3.43 us
    ppermute x1, starting transfers between devices, body(): lax.ppermute(bottom, 'wrap', [(k, (k + 1) % wraps) for k in range(wraps)])  1.92 us
    pallas_call x1, Pallas kernels, body(): call(setup_kernel, 2, [own_rows, own_rows, square, square], [pltpu.VMEM((...  1.49 us
    pallas_call x1, Pallas kernels, body(): call(outer_kernel, 7, [shaped(PLANES * 2 * HALO, COLS), shaped(owners, 8,...  1.31 us
  transfers between devices with their start and end apart: 4, of which 1 were waited for; matrix products, arithmetic and copies ran while one was open for 0% of the time, Pallas kernels for 12%

profile of v3, /device:TPU:1, one launch (start us, length us, event | category | flops | bytes accessed | tf_op | source)
XLA Modules:
  0.0 45.0 jit_solution(2651653216283525881)
XLA Ops:
  0.6 0.0 copy-start
  0.6 0.0 copy-start.1
  0.6 1.2 %bitcast_convert_fusion = f32[3072,128]{1,0:T(8,128)S(1)} fusion(bf16[3,32,32,128]{3,2,1,0:T(8,128)(2,1)} %param.3), kind=kLoop, calls=%fused_computation.1 | loop fusion | flops 393216 | bytes 2359296 | tf_op jit(solution)/shard_map/convert_element_type | solution.py:314
  1.9 0.0 copy-done
  1.9 0.0 copy-done.1
  1.9 0.1 pad_maximum_fusion.all_ref
  2.0 1.0 %shard_map.50 = (f32[32,4,128]{2,1,0:T(4,128)S(1)}, f32[32,4,128]{2,1,0:T(4,128)S(1)}) custom-call(f32[3136,128]{1,0:T(8,128)S(1)} %pad_maximum_fusion.all_ref), custom_call_target="tpu_custom_call" | custom-call | flops 1000 | bytes 1000 | tf_op jit(solution)/shard_map/pallas_call | solution.py:317
  3.0 4.5 %collective-permute-start = (f32[32,4,128]{2,1,0:T(4,128)S(1)}, f32[32,4,128]{2,1,0:T(4,128)S(1)}, u32[]{:S(2)}, u32[]{:S(2)}) collective-permute-start(f32[32,4,128]{2,1,0:T(4,128)S(1)} %get-tuple-element.22), channel_id=1, source_target_pairs={{1,2},{2,1},{3,4},{4,3},{5,6},{6,5},{7,8},{8,7},{9,10},{10,9},{11,... | collective-permute-start | bytes 196616 | tf_op jit(solution)/shard_map/ppermute | solution.py:319
  7.5 4.9 %collective-permute-start.1 = (f32[32,4,128]{2,1,0:T(4,128)S(1)}, f32[32,4,128]{2,1,0:T(4,128)S(1)}, u32[]{:S(2)}, u32[]{:S(2)}) collective-permute-start(f32[32,4,128]{2,1,0:T(4,128)S(1)} %shard_map.52.after_strip), channel_id=1, source_target_pairs={{0,1},{1,0},{2,3},{3,2},{4,5},{5,4},{6,7},{7,6},{8,9},{9,8},{10,11... | collective-permute-start | bytes 196616 | tf_op jit(solution)/shard_map/ppermute | solution.py:321
  12.5 1.5 %shard_map.53 = (f32[4352,128]{1,0:T(8,128)S(1)}, f32[4352,128]{1,0:T(8,128)S(1)}, f32[128,128]{1,0:T(8,128)S(1)}, f32[128,128]{1,0:T(8,128)S(1)}) custom-call(f32[3136,128]{1,0:T(8,128)S(1)} %pad_maximum_fusion.all_ref, f32[32,4,128]{2,1,0:T(4,128)S(1)} %shard_map.52.after_strip), custom_call_target="tpu_custom_call" | custom-call | flops 1000 | bytes 1000 | tf_op jit(solution)/shard_map/pallas_call | solution.py:322
  14.0 0.3 shard_map.54
  14.3 0.0 collective-permute-done.ref
  14.3 0.0 collective-permute-done.1.twin
  14.4 1.9 %collective-permute-start.2 = (f32[424,128]{1,0:T(8,128)S(1)}, f32[424,128]{1,0:T(8,128)S(1)}, u32[]{:S(2)}, u32[]{:S(2)}) collective-permute-start(f32[424,128]{1,0:T(8,128)S(1)} %get-tuple-element.27), channel_id=1, source_target_pairs={{0,16},{16,32},{32,48},{48,64},{64,80},{80,96},{96,112},{112,128},... | collective-permute-start | bytes 651272 | tf_op jit(solution)/shard_map/ppermute | solution.py:329
  16.3 10.7 %collective-permute-start.3 = (f32[424,128]{1,0:T(8,128)S(1)}, f32[424,128]{1,0:T(8,128)S(1)}, u32[]{:S(2)}, u32[]{:S(2)}) collective-permute-start(f32[424,128]{1,0:T(8,128)S(1)} %get-tuple-element.28), channel_id=1, source_target_pairs={{16,0},{32,16},{48,32},{64,48},{80,64},{96,80},{112,96},{128,112},... | collective-permute-start | bytes 651272 | tf_op jit(solution)/shard_map/ppermute | solution.py:330
  27.0 3.4 %shard_map.56 = (f32[4352,128]{1,0:T(8,128)S(1)}, f32[4352,128]{1,0:T(8,128)S(1)}, f32[1088,128]{1,0:T(8,128)S(1)}, f32[3072,128]{1,0:T(8,128)S(1)}, f32[128,128]{1,0:T(8,128)S(1)}) custom-call(f32[4352,128]{1,0:T(8,128)S(1)} %get-tuple-element.29.v_in, f32[4352,128]{1,0:T(8,128)S(1)} %get-tuple-element.30.f_in, ...), custom_call_target="tpu_custom_call", output_to_operand_aliasing={{0}: (0, {}), {1}: (1, {})} | custom-call | flops 20000000000 | bytes 1000 | tf_op jit(solution)/shard_map/pallas_call | solution.py:331
  30.5 0.0 collective-permute-done.2.above
  30.5 0.8 %collective-permute-done.3.below = f32[424,128]{1,0:T(8,128)S(1)} collective-permute-done((f32[424,128]{1,0:T(8,128)S(1)}, f32[424,128]{1,0:T(8,128)S(1)}, u32[]{:S(2)}, u32[]{:S(2)}) %collective-permute-start.3) | collective-permute-done | bytes 217120 | tf_op jit(solution)/shard_map/ppermute | solution.py:330
  31.3 1.3 %shard_map.57 = (f32[768,128]{1,0:T(8,128)S(1)}, f32[16,8,128]{2,1,0:T(8,128)S(1)}) custom-call(f32[424,128]{1,0:T(8,128)S(1)} %collective-permute-done.2.above, f32[424,128]{1,0:T(8,128)S(1)} %collective-permute-done.3.below, f32[4352,128]{1,0:T(8,128)S(1)} %get-tuple-element.33.v, f32[4352,128]{1,0:T(8,128)S(1)} %get-tuple-element.34.f, ...), custom_call_target="tpu_custom_call" | custom-call | flops 1000 | bytes 1000 | tf_op jit(solution)/shard_map/pallas_call | solution.py:339
  32.6 11.2 %all_to_all.5.got_ref = f32[16,8,128]{2,1,0:T(8,128)S(1)} all-to-all(f32[16,8,128]{2,1,0:T(8,128)S(1)} %get-tuple-element.37), channel_id=1, replica_groups=mesh['wrap'=32,'normal'=16] {'normal'}, dimensions={0} | all-to-all | bytes 131072 | tf_op jit(solution)/shard_map/all_to_all | solution.py:346
  43.8 1.1 %shard_map.58 = (bf16[96,32,128]{2,1,0:T(8,128)(2,1)}, f32[3,2,32]{2,1,0:T(2,128)}) custom-call(f32[16,8,128]{2,1,0:T(8,128)S(1)} %all_to_all.5.got_ref, f32[3072,128]{1,0:T(8,128)S(1)} %get-tuple-element.38.part, f32[768,128]{1,0:T(8,128)S(1)} %get-tuple-element.39.xe), custom_call_target="tpu_custom_call" | custom-call | flops 1000 | bytes 1000 | tf_op jit(solution)/shard_map/pallas_call | solution.py:347
  (3 shorter events, 0.1 us)
Async XLA Ops:
  0.6 1.3 %copy-start = (f32[32,128]{1,0:T(8,128)S(1)}, f32[32,128]{1,0:T(8,128)}, u32[]{:S(2)}) copy-start(f32[32,128]{1,0:T(8,128)} %param.5) | copy-start | bytes 49156
  0.6 1.3 %copy-start.1 = (f32[32,128]{1,0:T(8,128)S(1)}, f32[32,128]{1,0:T(8,128)}, u32[]{:S(2)}) copy-start(f32[32,128]{1,0:T(8,128)} %param.4) | copy-start | bytes 49156
  3.0 11.3 %collective-permute-start = (f32[32,4,128]{2,1,0:T(4,128)S(1)}, f32[32,4,128]{2,1,0:T(4,128)S(1)}, u32[]{:S(2)}, u32[]{:S(2)}) collective-permute-start(f32[32,4,128]{2,1,0:T(4,128)S(1)} %get-tuple-element.22), channel_id=1, source_target_pairs={{1,2},{2,1},{3,4},{4,3},{5,6},{6,5},{7,8},{8,7},{9,10},{10,9},{11,... | collective-permute-start | bytes 196616 | tf_op jit(solution)/shard_map/ppermute | solution.py:319
  7.5 6.8 %collective-permute-start.1 = (f32[32,4,128]{2,1,0:T(4,128)S(1)}, f32[32,4,128]{2,1,0:T(4,128)S(1)}, u32[]{:S(2)}, u32[]{:S(2)}) collective-permute-start(f32[32,4,128]{2,1,0:T(4,128)S(1)} %shard_map.52.after_strip), channel_id=1, source_target_pairs={{0,1},{1,0},{2,3},{3,2},{4,5},{5,4},{6,7},{7,6},{8,9},{9,8},{10,11... | collective-permute-start | bytes 196616 | tf_op jit(solution)/shard_map/ppermute | solution.py:321
  14.4 16.1 %collective-permute-start.2 = (f32[424,128]{1,0:T(8,128)S(1)}, f32[424,128]{1,0:T(8,128)S(1)}, u32[]{:S(2)}, u32[]{:S(2)}) collective-permute-start(f32[424,128]{1,0:T(8,128)S(1)} %get-tuple-element.27), channel_id=1, source_target_pairs={{0,16},{16,32},{32,48},{48,64},{64,80},{80,96},{96,112},{112,128},... | collective-permute-start | bytes 651272 | tf_op jit(solution)/shard_map/ppermute | solution.py:329
  16.3 15.0 %collective-permute-start.3 = (f32[424,128]{1,0:T(8,128)S(1)}, f32[424,128]{1,0:T(8,128)S(1)}, u32[]{:S(2)}, u32[]{:S(2)}) collective-permute-start(f32[424,128]{1,0:T(8,128)S(1)} %get-tuple-element.28), channel_id=1, source_target_pairs={{16,0},{32,16},{48,32},{64,48},{80,64},{96,80},{112,96},{128,112},... | collective-permute-start | bytes 651272 | tf_op jit(solution)/shard_map/ppermute | solution.py:330

commit v4 on v3

--- a/solution.py
+++ b/solution.py
@@ -24,7 +24,9 @@
 COEF_AT = PLANES * ROWS
 SPACING_AT = COEF_AT + ROWS
 ALL = SPACING_AT + ROWS
+PARTS = 2
 VMEM = pl.BlockSpec(memory_space=pltpu.VMEM)
+HBM = pl.BlockSpec(memory_space=pltpu.HBM)
 
 
 def nt(a, b):
@@ -39,7 +41,7 @@
     single = not isinstance(outs, (list, tuple))
     return pl.pallas_call(
         kernel,
-        in_specs=[VMEM] * ins,
+        in_specs=ins if isinstance(ins, list) else [VMEM] * ins,
         out_shape=outs,
         out_specs=VMEM if single else [VMEM] * len(outs),
         scratch_shapes=scratch,
@@ -126,7 +128,7 @@
     return high, value - high
 
 
-def rows_kernel(all_ref, after_setup, top_ref, bottom_ref):
+def rows_kernel(all_ref, after_twin, top_ref, bottom_ref):
     zero = jnp.zeros((HALO, COLS), F32)
     for ref, at in ((top_ref, 0), (bottom_ref, ROWS - HALO)):
         for k in range(HALO):
@@ -134,7 +136,23 @@
         ref[pl.ds(COEFS, 8), :] = jnp.concatenate([all_ref[pl.ds(COEF_AT + at, HALO), :], zero], axis=0)
 
 
-def strip_kernel(all_ref, cross_ref, twin_ref):
+def strip_kernel(x_hbm, coef_hbm, spacing_hbm, all_ref, cross_ref, twin_ref, x_ref, sems):
+    some = PLANES // PARTS
+    copies = [
+        pltpu.make_async_copy(coef_hbm, all_ref.at[pl.ds(COEF_AT, ROWS)], sems.at[PARTS]),
+        pltpu.make_async_copy(spacing_hbm, all_ref.at[pl.ds(SPACING_AT, ROWS)], sems.at[PARTS + 1]),
+    ]
+    for k in range(PARTS):
+        piece = pl.ds(k * some, some)
+        copies.append(pltpu.make_async_copy(x_hbm.at[piece], x_ref.at[piece], sems.at[k]))
+    for copy in copies[2:] + copies[:2]:
+        copy.start()
+    for k in range(PARTS):
+        copies[k + 2].wait()
+        piece = x_ref[pl.ds(k * some, some)].astype(F32)
+        all_ref[pl.ds(k * some * ROWS, some * ROWS), :] = piece.reshape(some * ROWS, COLS)
+    copies[0].wait()
+    copies[1].wait()
     row, col = iota((2 * HALO, COLS), 0), iota((2 * HALO, COLS), 1)
     pick = (col == jnp.where(row < HALO, row, COLS - 2 * HALO + row)).astype(BF16)
     even = lax.axis_index("normal") % 2 == 0
@@ -167,7 +185,7 @@
         bottom_ref[pl.ds(MAIN + 8 * r, 8), :] = strips[ROWS - HALO + r]
 
 
-def setup_kernel(all_ref, after_strip, v, f, weights, sums, ct):
+def setup_kernel(all_ref, after_corner, v, f, weights, sums, ct):
     select = selector()
     ring_coef = masked_ring(all_ref[pl.ds(COEF_AT, ROWS), :], ct)
     for r in range(ROWS):
@@ -311,21 +329,27 @@
 
 def body(adjoint_in, coef, spacing):
     wraps, owners = lax.axis_size("wrap"), lax.axis_size("normal")
-    everything = jnp.concatenate([adjoint_in.reshape(PLANES * ROWS, COLS).astype(F32), coef, spacing], axis=0)
     strip, square = shaped(ROWS, HALO, COLS), shaped(COLS, COLS)
     own_rows = shaped(ROWS * WIDE, COLS)
-    to_cross, to_twin = call(strip_kernel, 1, [strip, strip], [], 1_000)(everything)
+    x = adjoint_in.reshape(PLANES, ROWS, COLS)
+    everything, to_cross, to_twin = call(
+        strip_kernel,
+        [HBM] * 3,
+        [shaped(ALL, COLS), strip, strip],
+        [pltpu.VMEM((PLANES, ROWS, COLS), BF16), pltpu.SemaphoreType.DMA((PARTS + 2,))],
+        1_000,
+    )(*[pltpu.with_memory_space_constraint(a, pltpu.HBM) for a in (x, coef, spacing)])
     to_twin = call(pass_kernel, 1, strip, [], 1_000)(to_twin)
     cross = lax.ppermute(to_cross, "normal", [(k, k + 1 if k % 2 else k - 1) for k in range(1, owners - 1)])
     cross = call(pass_kernel, 1, strip, [], 1_000)(cross)
     twin = lax.ppermute(to_twin, "normal", [(k, k ^ 1) for k in range(owners)])
+    top, bottom = call(rows_kernel, 2, [shaped(MAIN, COLS)] * 2, [], 1_000)(everything, to_twin)
+    strips, top, bottom = call(corner_kernel, 4, [shaped(ROWS, 8, COLS), shaped(MSG, COLS), shaped(MSG, COLS)], [], 1_000)(
+        cross, twin, top, bottom
+    )
     v, f, weights, sums = call(
         setup_kernel, 2, [own_rows, own_rows, square, square], [pltpu.VMEM((WIDE, COLS), F32)], 1_000
-    )(everything, to_twin)
-    top, bottom = call(rows_kernel, 2, [shaped(MAIN, COLS)] * 2, [], 1_000)(everything, sums)
-    strips, top, bottom = call(corner_kernel, 4, [shaped(ROWS, 8, COLS), shaped(MSG, COLS), shaped(MSG, COLS)], [], 1_000)(
-        cross, twin, top, bottom
-    )
+    )(everything, strips)
     above = lax.ppermute(bottom, "wrap", [(k, (k + 1) % wraps) for k in range(wraps)])
     below = lax.ppermute(top, "wrap", [((k + 1) % wraps, k) for k in range(wraps)])
     v, f, kept, part, sums = call(

time: 45.3 us -> 44.6 us (0.985)
  other arithmetic: 1.35 us -> 0 us
  Pallas kernels: 8.68 us -> 9.9 us
  blocking collectives: 11.2 us -> 10.6 us
    convert_element_type x1 -> x0, other arithmetic: 1.25 us -> none  [body(): adjoint_in.reshape(PLANES * ROWS, COLS).astype(F32)]
    pallas_call x2, Pallas kernels: 1.25 us -> 2.46 us  [the longest x1 2.16 us: body(): call(strip_kernel, [HBM] * 3, [shaped(ALL, COLS), strip, strip], [pltpu.V...]
    ppermute x1, waiting for transfers between devices: 0.8 us -> 0.01 us  [body(): lax.ppermute(top, 'wrap', [((k + 1) % wraps, k) for k in range(wraps)])]
    all_to_all x1, blocking collectives: 11.2 us -> 10.6 us  [body(): got = lax.all_to_all(sums, 'normal', 0, 0, tiled=True)]
    ppermute x1, waiting for transfers between devices: 0.01 us -> 0.56 us  [body(): twin = lax.ppermute(to_twin, 'normal', [(k, k ^ 1) for k in range(owners)])]
where the time goes in v4:
time: 44.6 us; the launch traced here: 44.3 us
  starting transfers between devices  22.4 us (50%)
  blocking collectives  10.6 us (24%)
  Pallas kernels  9.9 us (22%)
  between operations  0.74 us (2%)
  waiting for transfers between devices  0.56 us (1%)
    ppermute x1, starting transfers between devices, body(): lax.ppermute(top, 'wrap', [((k + 1) % wraps, k) for k in range(wraps)])  10.9 us
    all_to_all x1, blocking collectives, body(): got = lax.all_to_all(sums, 'normal', 0, 0, tiled=True)  10.6 us
    ppermute x1, starting transfers between devices, body(): twin = lax.ppermute(to_twin, 'normal', [(k, k ^ 1) for k in range(owners)])  4.94 us
    ppermute x1, starting transfers between devices, body(): lax.ppermute(to_cross, 'normal', [(k, k + 1 if k % 2 else k - 1) for k in...  4.51 us
    pallas_call x1, Pallas kernels, body(): call(inner_kernel, 5, [own_rows, own_rows, shaped(2 * HALO * WIDE, COLS),...  3.43 us
    pallas_call x1, Pallas kernels, body(): call(strip_kernel, [HBM] * 3, [shaped(ALL, COLS), strip, strip], [pltpu.V...  2.16 us
    ppermute x1, starting transfers between devices, body(): lax.ppermute(bottom, 'wrap', [(k, (k + 1) % wraps) for k in range(wraps)])  2.14 us
    pallas_call x1, Pallas kernels, body(): call(setup_kernel, 2, [own_rows, own_rows, square, square], [pltpu.VMEM((...  1.49 us
  transfers between devices with their start and end apart: 4, of which 1 were waited for; matrix products, arithmetic and copies ran while one was open for 0% of the time, Pallas kernels for 12%

profile of v4, /device:TPU:1, one launch (start us, length us, event | category | flops | bytes accessed | tf_op | source)
XLA Modules:
  0.0 44.3 jit_solution(17858152319457526820)
XLA Ops:
  0.6 2.2 %shard_map.50 = (f32[3136,128]{1,0:T(8,128)S(1)}, f32[32,4,128]{2,1,0:T(4,128)S(1)}, f32[32,4,128]{2,1,0:T(4,128)S(1)}) custom-call(bf16[96,32,128]{2,1,0:T(8,128)(2,1)} %bitcast.2, f32[32,128]{1,0:T(8,128)} %coef_hbm.1, f32[32,128]{1,0:T(8,128)} %spacing_hbm.1), custom_call_target="tpu_custom_call" | custom-call | flops 1000 | bytes 1000 | tf_op jit(solution)/shard_map/pallas_call | solution.py:335
  2.8 4.5 %collective-permute-start = (f32[32,4,128]{2,1,0:T(4,128)S(1)}, f32[32,4,128]{2,1,0:T(4,128)S(1)}, u32[]{:S(2)}, u32[]{:S(2)}) collective-permute-start(f32[32,4,128]{2,1,0:T(4,128)S(1)} %get-tuple-element.23), channel_id=1, source_target_pairs={{1,2},{2,1},{3,4},{4,3},{5,6},{6,5},{7,8},{8,7},{9,10},{10,9},{11,... | collective-permute-start | bytes 196616 | tf_op jit(solution)/shard_map/ppermute | solution.py:343
  7.3 4.9 %collective-permute-start.1 = (f32[32,4,128]{2,1,0:T(4,128)S(1)}, f32[32,4,128]{2,1,0:T(4,128)S(1)}, u32[]{:S(2)}, u32[]{:S(2)}) collective-permute-start(f32[32,4,128]{2,1,0:T(4,128)S(1)} %shard_map.52.after_twin), channel_id=1, source_target_pairs={{0,1},{1,0},{2,3},{3,2},{4,5},{5,4},{6,7},{7,6},{8,9},{9,8},{10,11... | collective-permute-start | bytes 196616 | tf_op jit(solution)/shard_map/ppermute | solution.py:345
  12.3 0.3 shard_map.53
  12.6 0.0 collective-permute-done.ref
  12.6 0.6 %collective-permute-done.1.twin = f32[32,4,128]{2,1,0:T(4,128)S(1)} collective-permute-done((f32[32,4,128]{2,1,0:T(4,128)S(1)}, f32[32,4,128]{2,1,0:T(4,128)S(1)}, u32[]{:S(2)}, u32[]{:S(2)}) %collective-permute-start.1) | collective-permute-done | bytes 65568 | tf_op jit(solution)/shard_map/ppermute | solution.py:345
  13.2 2.1 %collective-permute-start.2 = (f32[424,128]{1,0:T(8,128)S(1)}, f32[424,128]{1,0:T(8,128)S(1)}, u32[]{:S(2)}, u32[]{:S(2)}) collective-permute-start(f32[424,128]{1,0:T(8,128)S(1)} %get-tuple-element.28), channel_id=1, source_target_pairs={{0,16},{16,32},{32,48},{48,64},{64,80},{80,96},{96,112},{112,128},... | collective-permute-start | bytes 651272 | tf_op jit(solution)/shard_map/ppermute | solution.py:353
  15.4 10.9 %collective-permute-start.3 = (f32[424,128]{1,0:T(8,128)S(1)}, f32[424,128]{1,0:T(8,128)S(1)}, u32[]{:S(2)}, u32[]{:S(2)}) collective-permute-start(f32[424,128]{1,0:T(8,128)S(1)} %get-tuple-element.29), channel_id=1, source_target_pairs={{16,0},{32,16},{48,32},{64,48},{80,64},{96,80},{112,96},{128,112},... | collective-permute-start | bytes 651272 | tf_op jit(solution)/shard_map/ppermute | solution.py:354
  26.2 1.5 %shard_map.55 = (f32[4352,128]{1,0:T(8,128)S(1)}, f32[4352,128]{1,0:T(8,128)S(1)}, f32[128,128]{1,0:T(8,128)S(1)}, f32[128,128]{1,0:T(8,128)S(1)}) custom-call(f32[3136,128]{1,0:T(8,128)S(1)} %get-tuple-element.25.all_ref, f32[32,8,128]{2,1,0:T(8,128)S(1)} %get-tuple-element.30.after_corner.strips), custom_call_target="tpu_custom_call" | custom-call | flops 1000 | bytes 1000 | tf_op jit(solution)/shard_map/pallas_call | solution.py:350
  27.7 3.4 %shard_map.56 = (f32[4352,128]{1,0:T(8,128)S(1)}, f32[4352,128]{1,0:T(8,128)S(1)}, f32[1088,128]{1,0:T(8,128)S(1)}, f32[3072,128]{1,0:T(8,128)S(1)}, f32[128,128]{1,0:T(8,128)S(1)}) custom-call(f32[4352,128]{1,0:T(8,128)S(1)} %get-tuple-element.31.v_in, f32[4352,128]{1,0:T(8,128)S(1)} %get-tuple-element.32.f_in, ...), custom_call_target="tpu_custom_call", output_to_operand_aliasing={{0}: (0, {}), {1}: (1, {})} | custom-call | flops 20000000000 | bytes 1000 | tf_op jit(solution)/shard_map/pallas_call | solution.py:355
  31.2 0.0 collective-permute-done.2.above
  31.2 0.0 collective-permute-done.3.below
  31.2 1.3 %shard_map.57 = (f32[768,128]{1,0:T(8,128)S(1)}, f32[16,8,128]{2,1,0:T(8,128)S(1)}) custom-call(f32[424,128]{1,0:T(8,128)S(1)} %collective-permute-done.2.above, f32[424,128]{1,0:T(8,128)S(1)} %collective-permute-done.3.below, f32[4352,128]{1,0:T(8,128)S(1)} %get-tuple-element.35.v, f32[4352,128]{1,0:T(8,128)S(1)} %get-tuple-element.36.f, ...), custom_call_target="tpu_custom_call" | custom-call | flops 1000 | bytes 1000 | tf_op jit(solution)/shard_map/pallas_call | solution.py:363
  32.5 10.6 %all_to_all.5.got_ref = f32[16,8,128]{2,1,0:T(8,128)S(1)} all-to-all(f32[16,8,128]{2,1,0:T(8,128)S(1)} %get-tuple-element.39), channel_id=1, replica_groups=mesh['wrap'=32,'normal'=16] {'normal'}, dimensions={0} | all-to-all | bytes 131072 | tf_op jit(solution)/shard_map/all_to_all | solution.py:370
  43.1 1.2 %shard_map.58 = (bf16[96,32,128]{2,1,0:T(8,128)(2,1)}, f32[3,2,32]{2,1,0:T(2,128)}) custom-call(f32[16,8,128]{2,1,0:T(8,128)S(1)} %all_to_all.5.got_ref, f32[3072,128]{1,0:T(8,128)S(1)} %get-tuple-element.40.part, f32[768,128]{1,0:T(8,128)S(1)} %get-tuple-element.41.xe), custom_call_target="tpu_custom_call" | custom-call | flops 1000 | bytes 1000 | tf_op jit(solution)/shard_map/pallas_call | solution.py:371
  (3 shorter events, 0.1 us)
Async XLA Ops:
  2.8 9.8 %collective-permute-start = (f32[32,4,128]{2,1,0:T(4,128)S(1)}, f32[32,4,128]{2,1,0:T(4,128)S(1)}, u32[]{:S(2)}, u32[]{:S(2)}) collective-permute-start(f32[32,4,128]{2,1,0:T(4,128)S(1)} %get-tuple-element.23), channel_id=1, source_target_pairs={{1,2},{2,1},{3,4},{4,3},{5,6},{6,5},{7,8},{8,7},{9,10},{10,9},{11,... | collective-permute-start | bytes 196616 | tf_op jit(solution)/shard_map/ppermute | solution.py:343
  7.3 5.8 %collective-permute-start.1 = (f32[32,4,128]{2,1,0:T(4,128)S(1)}, f32[32,4,128]{2,1,0:T(4,128)S(1)}, u32[]{:S(2)}, u32[]{:S(2)}) collective-permute-start(f32[32,4,128]{2,1,0:T(4,128)S(1)} %shard_map.52.after_twin), channel_id=1, source_target_pairs={{0,1},{1,0},{2,3},{3,2},{4,5},{5,4},{6,7},{7,6},{8,9},{9,8},{10,11... | collective-permute-start | bytes 196616 | tf_op jit(solution)/shard_map/ppermute | solution.py:345
  13.2 17.9 %collective-permute-start.2 = (f32[424,128]{1,0:T(8,128)S(1)}, f32[424,128]{1,0:T(8,128)S(1)}, u32[]{:S(2)}, u32[]{:S(2)}) collective-permute-start(f32[424,128]{1,0:T(8,128)S(1)} %get-tuple-element.28), channel_id=1, source_target_pairs={{0,16},{16,32},{32,48},{48,64},{64,80},{80,96},{96,112},{112,128},... | collective-permute-start | bytes 651272 | tf_op jit(solution)/shard_map/ppermute | solution.py:353
  15.4 15.8 %collective-permute-start.3 = (f32[424,128]{1,0:T(8,128)S(1)}, f32[424,128]{1,0:T(8,128)S(1)}, u32[]{:S(2)}, u32[]{:S(2)}) collective-permute-start(f32[424,128]{1,0:T(8,128)S(1)} %get-tuple-element.29), channel_id=1, source_target_pairs={{16,0},{32,16},{48,32},{64,48},{80,64},{96,80},{112,96},{128,112},... | collective-permute-start | bytes 651272 | tf_op jit(solution)/shard_map/ppermute | solution.py:354

commit v5 on v4

--- a/solution.py
+++ b/solution.py
@@ -19,6 +19,7 @@
 COEFS = HALO * PLANES
 MAIN = COEFS + 8
 MSG = MAIN + 8 * HALO
+SPARE = 3 * 8
 F32 = jnp.float32
 BF16 = jnp.bfloat16
 COEF_AT = PLANES * ROWS
@@ -294,8 +295,8 @@
 
 
 def final_kernel(got_ref, part, xe, out_ref, wall_ref):
-    tiles = part[...].reshape(PLANES, ROWS // 8, 8, COLS)
-    ends = xe[...].reshape(PLANES, 8, COLS)
+    tiles = part[pl.ds(0, PLANES * ROWS), :].reshape(PLANES, ROWS // 8, 8, COLS)
+    ends = xe[pl.ds(0, PLANES * 8), :].reshape(PLANES, 8, COLS)
     near = iota((PLANES, 8, COLS), 1) < HALO
     head = jnp.where(near, ends, tiles[:, 0])
     tail = jnp.where(near, tiles[:, 3], ends)
@@ -324,13 +325,13 @@
 
 
 def lines(count):
-    return pltpu.VMEM((count * WIDE, COLS), F32)
+    return pltpu.VMEM((count * WIDE + SPARE, COLS), F32)
 
 
 def body(adjoint_in, coef, spacing):
     wraps, owners = lax.axis_size("wrap"), lax.axis_size("normal")
     strip, square = shaped(ROWS, HALO, COLS), shaped(COLS, COLS)
-    own_rows = shaped(ROWS * WIDE, COLS)
+    own_rows = shaped(ROWS * WIDE + SPARE, COLS)
     x = adjoint_in.reshape(PLANES, ROWS, COLS)
     everything, to_cross, to_twin = call(
         strip_kernel,
@@ -348,14 +349,14 @@
         cross, twin, top, bottom
     )
     v, f, weights, sums = call(
-        setup_kernel, 2, [own_rows, own_rows, square, square], [pltpu.VMEM((WIDE, COLS), F32)], 1_000
+        setup_kernel, 2, [own_rows, own_rows, square, square], [pltpu.VMEM((WIDE + SPARE, COLS), F32)], 1_000
     )(everything, strips)
     above = lax.ppermute(bottom, "wrap", [(k, (k + 1) % wraps) for k in range(wraps)])
     below = lax.ppermute(top, "wrap", [((k + 1) % wraps, k) for k in range(wraps)])
     v, f, kept, part, sums = call(
         inner_kernel,
         5,
-        [own_rows, own_rows, shaped(2 * HALO * WIDE, COLS), shaped(PLANES * ROWS, COLS), square],
+        [own_rows, own_rows, shaped(2 * HALO * WIDE, COLS), shaped(PLANES * ROWS + ROWS, COLS), square],
         [],
         20_000_000_000,
         {0: 0, 1: 1},
@@ -363,8 +364,8 @@
     ends, sums = call(
         outer_kernel,
         7,
-        [shaped(PLANES * 2 * HALO, COLS), shaped(owners, 8, COLS)],
-        [lines(4 * HALO), lines(4 * HALO), pltpu.VMEM((WIDE, COLS), F32), lines(2 * HALO), pltpu.VMEM((COLS, COLS), F32)],
+        [shaped(PLANES * 2 * HALO + 2 * HALO, COLS), shaped(owners, 8, COLS)],
+        [lines(4 * HALO), lines(4 * HALO), pltpu.VMEM((WIDE + SPARE, COLS), F32), lines(2 * HALO), pltpu.VMEM((COLS, COLS), F32)],
         1_000,
     )(above, below, v, f, kept, sums, weights)
     got = lax.all_to_all(sums, "normal", 0, 0, tiled=True)

time: 44.6 us -> 44.7 us (level)
  no operation moved by 1% of the time
where the time goes in v5:
time: 44.7 us; the launch traced here: 44.5 us
  starting transfers between devices  22.4 us (50%)
  blocking collectives  10.6 us (24%)
  Pallas kernels  10.1 us (23%)
  between operations  0.74 us (2%)
  waiting for transfers between devices  0.56 us (1%)
    ppermute x1, starting transfers between devices, body(): lax.ppermute(top, 'wrap', [((k + 1) % wraps, k) for k in range(wraps)])  10.9 us
    all_to_all x1, blocking collectives, body(): got = lax.all_to_all(sums, 'normal', 0, 0, tiled=True)  10.6 us
    ppermute x1, starting transfers between devices, body(): twin = lax.ppermute(to_twin, 'normal', [(k, k ^ 1) for k in range(owners)])  4.94 us
    ppermute x1, starting transfers between devices, body(): lax.ppermute(to_cross, 'normal', [(k, k + 1 if k % 2 else k - 1) for k in...  4.51 us
    pallas_call x1, Pallas kernels, body(): call(inner_kernel, 5, [own_rows, own_rows, shaped(2 * HALO * WIDE, COLS),...  3.5 us
    pallas_call x1, Pallas kernels, body(): call(strip_kernel, [HBM] * 3, [shaped(ALL, COLS), strip, strip], [pltpu.V...  2.16 us
    ppermute x1, starting transfers between devices, body(): lax.ppermute(bottom, 'wrap', [(k, (k + 1) % wraps) for k in range(wraps)])  2.14 us
    pallas_call x1, Pallas kernels, body(): call(setup_kernel, 2, [own_rows, own_rows, square, square], [pltpu.VMEM((...  1.53 us
  transfers between devices with their start and end apart: 4, of which 1 were waited for; matrix products, arithmetic and copies ran while one was open for 0% of the time, Pallas kernels for 12%

profile of v5, /device:TPU:1, one launch (start us, length us, event | category | flops | bytes accessed | tf_op | source)
XLA Modules:
  0.0 44.5 jit_solution(12166126652555101617)
XLA Ops:
  0.6 2.2 %shard_map.50 = (f32[3136,128]{1,0:T(8,128)S(1)}, f32[32,4,128]{2,1,0:T(4,128)S(1)}, f32[32,4,128]{2,1,0:T(4,128)S(1)}) custom-call(bf16[96,32,128]{2,1,0:T(8,128)(2,1)} %bitcast.2, f32[32,128]{1,0:T(8,128)} %coef_hbm.1, f32[32,128]{1,0:T(8,128)} %spacing_hbm.1), custom_call_target="tpu_custom_call" | custom-call | flops 1000 | bytes 1000 | tf_op jit(solution)/shard_map/pallas_call | solution.py:336
  2.8 4.5 %collective-permute-start = (f32[32,4,128]{2,1,0:T(4,128)S(1)}, f32[32,4,128]{2,1,0:T(4,128)S(1)}, u32[]{:S(2)}, u32[]{:S(2)}) collective-permute-start(f32[32,4,128]{2,1,0:T(4,128)S(1)} %get-tuple-element.23), channel_id=1, source_target_pairs={{1,2},{2,1},{3,4},{4,3},{5,6},{6,5},{7,8},{8,7},{9,10},{10,9},{11,... | collective-permute-start | bytes 196616 | tf_op jit(solution)/shard_map/ppermute | solution.py:344
  7.3 4.9 %collective-permute-start.1 = (f32[32,4,128]{2,1,0:T(4,128)S(1)}, f32[32,4,128]{2,1,0:T(4,128)S(1)}, u32[]{:S(2)}, u32[]{:S(2)}) collective-permute-start(f32[32,4,128]{2,1,0:T(4,128)S(1)} %shard_map.52.after_twin), channel_id=1, source_target_pairs={{0,1},{1,0},{2,3},{3,2},{4,5},{5,4},{6,7},{7,6},{8,9},{9,8},{10,11... | collective-permute-start | bytes 196616 | tf_op jit(solution)/shard_map/ppermute | solution.py:346
  12.3 0.3 shard_map.53
  12.6 0.0 collective-permute-done.ref
  12.6 0.6 %collective-permute-done.1.twin = f32[32,4,128]{2,1,0:T(4,128)S(1)} collective-permute-done((f32[32,4,128]{2,1,0:T(4,128)S(1)}, f32[32,4,128]{2,1,0:T(4,128)S(1)}, u32[]{:S(2)}, u32[]{:S(2)}) %collective-permute-start.1) | collective-permute-done | bytes 65568 | tf_op jit(solution)/shard_map/ppermute | solution.py:346
  13.2 2.1 %collective-permute-start.2 = (f32[424,128]{1,0:T(8,128)S(1)}, f32[424,128]{1,0:T(8,128)S(1)}, u32[]{:S(2)}, u32[]{:S(2)}) collective-permute-start(f32[424,128]{1,0:T(8,128)S(1)} %get-tuple-element.28), channel_id=1, source_target_pairs={{0,16},{16,32},{32,48},{48,64},{64,80},{80,96},{96,112},{112,128},... | collective-permute-start | bytes 651272 | tf_op jit(solution)/shard_map/ppermute | solution.py:354
  15.4 10.9 %collective-permute-start.3 = (f32[424,128]{1,0:T(8,128)S(1)}, f32[424,128]{1,0:T(8,128)S(1)}, u32[]{:S(2)}, u32[]{:S(2)}) collective-permute-start(f32[424,128]{1,0:T(8,128)S(1)} %get-tuple-element.29), channel_id=1, source_target_pairs={{16,0},{32,16},{48,32},{64,48},{80,64},{96,80},{112,96},{128,112},... | collective-permute-start | bytes 651272 | tf_op jit(solution)/shard_map/ppermute | solution.py:355
  26.2 1.5 %shard_map.55 = (f32[4376,128]{1,0:T(8,128)S(1)}, f32[4376,128]{1,0:T(8,128)S(1)}, f32[128,128]{1,0:T(8,128)S(1)}, f32[128,128]{1,0:T(8,128)S(1)}) custom-call(f32[3136,128]{1,0:T(8,128)S(1)} %get-tuple-element.25.all_ref, f32[32,8,128]{2,1,0:T(8,128)S(1)} %get-tuple-element.30.after_corner.strips), custom_call_target="tpu_custom_call" | custom-call | flops 1000 | bytes 1000 | tf_op jit(solution)/shard_map/pallas_call | solution.py:351
  27.8 3.5 %shard_map.56 = (f32[4376,128]{1,0:T(8,128)S(1)}, f32[4376,128]{1,0:T(8,128)S(1)}, f32[1088,128]{1,0:T(8,128)S(1)}, f32[3104,128]{1,0:T(8,128)S(1)}, f32[128,128]{1,0:T(8,128)S(1)}) custom-call(f32[4376,128]{1,0:T(8,128)S(1)} %get-tuple-element.31.v_in, f32[4376,128]{1,0:T(8,128)S(1)} %get-tuple-element.32.f_in, ...), custom_call_target="tpu_custom_call", output_to_operand_aliasing={{0}: (0, {}), {1}: (1, {})} | custom-call | flops 20000000000 | bytes 1000 | tf_op jit(solution)/shard_map/pallas_call | solution.py:356
  31.3 0.0 collective-permute-done.2.above
  31.3 0.0 collective-permute-done.3.below
  31.3 1.3 %shard_map.57 = (f32[776,128]{1,0:T(8,128)S(1)}, f32[16,8,128]{2,1,0:T(8,128)S(1)}) custom-call(f32[424,128]{1,0:T(8,128)S(1)} %collective-permute-done.2.above, f32[424,128]{1,0:T(8,128)S(1)} %collective-permute-done.3.below, f32[4376,128]{1,0:T(8,128)S(1)} %get-tuple-element.35.v, f32[4376,128]{1,0:T(8,128)S(1)} %get-tuple-element.36.f, ...), custom_call_target="tpu_custom_call" | custom-call | flops 1000 | bytes 1000 | tf_op jit(solution)/shard_map/pallas_call | solution.py:364
  32.6 10.6 %all_to_all.5.got_ref = f32[16,8,128]{2,1,0:T(8,128)S(1)} all-to-all(f32[16,8,128]{2,1,0:T(8,128)S(1)} %get-tuple-element.39), channel_id=1, replica_groups=mesh['wrap'=32,'normal'=16] {'normal'}, dimensions={0} | all-to-all | bytes 131072 | tf_op jit(solution)/shard_map/all_to_all | solution.py:371
  43.3 1.2 %shard_map.58 = (bf16[96,32,128]{2,1,0:T(8,128)(2,1)}, f32[3,2,32]{2,1,0:T(2,128)}) custom-call(f32[16,8,128]{2,1,0:T(8,128)S(1)} %all_to_all.5.got_ref, f32[3104,128]{1,0:T(8,128)S(1)} %get-tuple-element.40.part, f32[776,128]{1,0:T(8,128)S(1)} %get-tuple-element.41.xe), custom_call_target="tpu_custom_call" | custom-call | flops 1000 | bytes 1000 | tf_op jit(solution)/shard_map/pallas_call | solution.py:372
  (3 shorter events, 0.1 us)
Async XLA Ops:
  2.8 9.8 %collective-permute-start = (f32[32,4,128]{2,1,0:T(4,128)S(1)}, f32[32,4,128]{2,1,0:T(4,128)S(1)}, u32[]{:S(2)}, u32[]{:S(2)}) collective-permute-start(f32[32,4,128]{2,1,0:T(4,128)S(1)} %get-tuple-element.23), channel_id=1, source_target_pairs={{1,2},{2,1},{3,4},{4,3},{5,6},{6,5},{7,8},{8,7},{9,10},{10,9},{11,... | collective-permute-start | bytes 196616 | tf_op jit(solution)/shard_map/ppermute | solution.py:344
  7.3 5.8 %collective-permute-start.1 = (f32[32,4,128]{2,1,0:T(4,128)S(1)}, f32[32,4,128]{2,1,0:T(4,128)S(1)}, u32[]{:S(2)}, u32[]{:S(2)}) collective-permute-start(f32[32,4,128]{2,1,0:T(4,128)S(1)} %shard_map.52.after_twin), channel_id=1, source_target_pairs={{0,1},{1,0},{2,3},{3,2},{4,5},{5,4},{6,7},{7,6},{8,9},{9,8},{10,11... | collective-permute-start | bytes 196616 | tf_op jit(solution)/shard_map/ppermute | solution.py:346
  13.2 18.1 %collective-permute-start.2 = (f32[424,128]{1,0:T(8,128)S(1)}, f32[424,128]{1,0:T(8,128)S(1)}, u32[]{:S(2)}, u32[]{:S(2)}) collective-permute-start(f32[424,128]{1,0:T(8,128)S(1)} %get-tuple-element.28), channel_id=1, source_target_pairs={{0,16},{16,32},{32,48},{48,64},{64,80},{80,96},{96,112},{112,128},... | collective-permute-start | bytes 651272 | tf_op jit(solution)/shard_map/ppermute | solution.py:354
  15.4 15.9 %collective-permute-start.3 = (f32[424,128]{1,0:T(8,128)S(1)}, f32[424,128]{1,0:T(8,128)S(1)}, u32[]{:S(2)}, u32[]{:S(2)}) collective-permute-start(f32[424,128]{1,0:T(8,128)S(1)} %get-tuple-element.29), channel_id=1, source_target_pairs={{16,0},{32,16},{48,32},{64,48},{80,64},{96,80},{112,96},{128,112},... | collective-permute-start | bytes 651272 | tf_op jit(solution)/shard_map/ppermute | solution.py:355

commit v6 on v5

--- a/solution.py
+++ b/solution.py
@@ -18,7 +18,7 @@
 STRIP_AT = WIDE - 7 * 8 - 1
 COEFS = HALO * PLANES
 MAIN = COEFS + 8
-MSG = MAIN + 8 * HALO
+MSG = MAIN + 8 * (HALO - 1)
 SPARE = 3 * 8
 F32 = jnp.float32
 BF16 = jnp.bfloat16
@@ -181,9 +181,9 @@
     strips_ref[...] = strips
     top_ref[pl.ds(0, MAIN), :] = top[...]
     bottom_ref[pl.ds(0, MAIN), :] = bottom[...]
-    for r in range(HALO):
+    for r in range(HALO - 1):
         top_ref[pl.ds(MAIN + 8 * r, 8), :] = strips[r]
-        bottom_ref[pl.ds(MAIN + 8 * r, 8), :] = strips[ROWS - HALO + r]
+        bottom_ref[pl.ds(MAIN + 8 * r, 8), :] = strips[ROWS - HALO + 1 + r]
 
 
 def setup_kernel(all_ref, after_corner, v, f, weights, sums, ct):
@@ -225,7 +225,7 @@
         here = line_of(f, low) * value
         put_line(kept, sweep, here)
         held = (opened(value, here, line_of(f, low - 1) * line_of(v, low - 1)), here)
-        held = lax.fori_loop(low, high, step, held, unroll=4)
+        held = lax.fori_loop(low, high, step, held, unroll=8)
         put_line(kept, HALO + sweep, held[1])
         put(v, high, held[0] + line_of(f, high + 1) * line_of(v, high + 1))
 
@@ -242,10 +242,10 @@
     select = selector()
     ring_coef = masked_ring(jnp.concatenate([above[pl.ds(COEFS, HALO), :], below[pl.ds(COEFS, HALO), :]], axis=0), ct)
     for k in range(HALO):
-        for message, at, c in ((above, k, k), (below, 3 * HALO + k, HALO + k)):
+        for message, at, c, sent in ((above, k, k, k - 1), (below, 3 * HALO + k, HALO + k, k)):
             hv[pl.ds(at * WIDE, WIDE), :] = to_lanes(select, message[pl.ds(k * PLANES, PLANES), :])
             hf[pl.ds(at * WIDE, WIDE), :] = jnp.broadcast_to(ring_coef[:, c : c + 1], (WIDE, COLS))
-            strip = message[pl.ds(MAIN + 8 * k, 8), :]
+            strip = message[pl.ds(MAIN + 8 * sent, 8), :] if 0 <= sent < HALO - 1 else jnp.zeros((8, COLS), F32)
             put_strip(hv, at, strip)
             put_strip(hf, at, coef_strip(strip))
     own = {HALO + k: k for k in range(HALO)} | {2 * HALO + k: ROWS - HALO + k for k in range(HALO)}

time: 44.7 us -> 44.7 us (level)
  no operation moved by 1% of the time
where the time goes in v6:
time: 44.7 us; the launch traced here: 44.4 us
  starting transfers between devices  22.4 us (50%)
  blocking collectives  10.6 us (24%)
  Pallas kernels  10 us (22%)
  between operations  0.74 us (2%)
  waiting for transfers between devices  0.56 us (1%)
    ppermute x1, starting transfers between devices, body(): lax.ppermute(top, 'wrap', [((k + 1) % wraps, k) for k in range(wraps)])  10.9 us
    all_to_all x1, blocking collectives, body(): got = lax.all_to_all(sums, 'normal', 0, 0, tiled=True)  10.6 us
    ppermute x1, starting transfers between devices, body(): twin = lax.ppermute(to_twin, 'normal', [(k, k ^ 1) for k in range(owners)])  4.94 us
    ppermute x1, starting transfers between devices, body(): lax.ppermute(to_cross, 'normal', [(k, k + 1 if k % 2 else k - 1) for k in...  4.51 us
    pallas_call x1, Pallas kernels, body(): call(inner_kernel, 5, [own_rows, own_rows, shaped(2 * HALO * WIDE, COLS),...  3.46 us
    pallas_call x1, Pallas kernels, body(): call(strip_kernel, [HBM] * 3, [shaped(ALL, COLS), strip, strip], [pltpu.V...  2.16 us
    ppermute x1, starting transfers between devices, body(): lax.ppermute(bottom, 'wrap', [(k, (k + 1) % wraps) for k in range(wraps)])  2.14 us
    pallas_call x1, Pallas kernels, body(): call(setup_kernel, 2, [own_rows, own_rows, square, square], [pltpu.VMEM((...  1.52 us
  transfers between devices with their start and end apart: 4, of which 1 were waited for; matrix products, arithmetic and copies ran while one was open for 0% of the time, Pallas kernels for 12%

profile of v6, /device:TPU:1, one launch (start us, length us, event | category | flops | bytes accessed | tf_op | source)
XLA Modules:
  0.0 44.4 jit_solution(5525237435758003541)
XLA Ops:
  0.6 2.2 %shard_map.50 = (f32[3136,128]{1,0:T(8,128)S(1)}, f32[32,4,128]{2,1,0:T(4,128)S(1)}, f32[32,4,128]{2,1,0:T(4,128)S(1)}) custom-call(bf16[96,32,128]{2,1,0:T(8,128)(2,1)} %bitcast.2, f32[32,128]{1,0:T(8,128)} %coef_hbm.1, f32[32,128]{1,0:T(8,128)} %spacing_hbm.1), custom_call_target="tpu_custom_call" | custom-call | flops 1000 | bytes 1000 | tf_op jit(solution)/shard_map/pallas_call | solution.py:336
  2.8 4.5 %collective-permute-start = (f32[32,4,128]{2,1,0:T(4,128)S(1)}, f32[32,4,128]{2,1,0:T(4,128)S(1)}, u32[]{:S(2)}, u32[]{:S(2)}) collective-permute-start(f32[32,4,128]{2,1,0:T(4,128)S(1)} %get-tuple-element.23), channel_id=1, source_target_pairs={{1,2},{2,1},{3,4},{4,3},{5,6},{6,5},{7,8},{8,7},{9,10},{10,9},{11,... | collective-permute-start | bytes 196616 | tf_op jit(solution)/shard_map/ppermute | solution.py:344
  7.3 4.9 %collective-permute-start.1 = (f32[32,4,128]{2,1,0:T(4,128)S(1)}, f32[32,4,128]{2,1,0:T(4,128)S(1)}, u32[]{:S(2)}, u32[]{:S(2)}) collective-permute-start(f32[32,4,128]{2,1,0:T(4,128)S(1)} %shard_map.52.after_twin), channel_id=1, source_target_pairs={{0,1},{1,0},{2,3},{3,2},{4,5},{5,4},{6,7},{7,6},{8,9},{9,8},{10,11... | collective-permute-start | bytes 196616 | tf_op jit(solution)/shard_map/ppermute | solution.py:346
  12.3 0.3 shard_map.53
  12.6 0.0 collective-permute-done.ref
  12.6 0.6 %collective-permute-done.1.twin = f32[32,4,128]{2,1,0:T(4,128)S(1)} collective-permute-done((f32[32,4,128]{2,1,0:T(4,128)S(1)}, f32[32,4,128]{2,1,0:T(4,128)S(1)}, u32[]{:S(2)}, u32[]{:S(2)}) %collective-permute-start.1) | collective-permute-done | bytes 65568 | tf_op jit(solution)/shard_map/ppermute | solution.py:346
  13.2 2.1 %collective-permute-start.2 = (f32[416,128]{1,0:T(8,128)S(1)}, f32[416,128]{1,0:T(8,128)S(1)}, u32[]{:S(2)}, u32[]{:S(2)}) collective-permute-start(f32[416,128]{1,0:T(8,128)S(1)} %get-tuple-element.28), channel_id=1, source_target_pairs={{0,16},{16,32},{32,48},{48,64},{64,80},{80,96},{96,112},{112,128},... | collective-permute-start | bytes 638984 | tf_op jit(solution)/shard_map/ppermute | solution.py:354
  15.4 10.9 %collective-permute-start.3 = (f32[416,128]{1,0:T(8,128)S(1)}, f32[416,128]{1,0:T(8,128)S(1)}, u32[]{:S(2)}, u32[]{:S(2)}) collective-permute-start(f32[416,128]{1,0:T(8,128)S(1)} %get-tuple-element.29), channel_id=1, source_target_pairs={{16,0},{32,16},{48,32},{64,48},{80,64},{96,80},{112,96},{128,112},... | collective-permute-start | bytes 638984 | tf_op jit(solution)/shard_map/ppermute | solution.py:355
  26.2 1.5 %shard_map.55 = (f32[4376,128]{1,0:T(8,128)S(1)}, f32[4376,128]{1,0:T(8,128)S(1)}, f32[128,128]{1,0:T(8,128)S(1)}, f32[128,128]{1,0:T(8,128)S(1)}) custom-call(f32[3136,128]{1,0:T(8,128)S(1)} %get-tuple-element.25.all_ref, f32[32,8,128]{2,1,0:T(8,128)S(1)} %get-tuple-element.30.after_corner.strips), custom_call_target="tpu_custom_call" | custom-call | flops 1000 | bytes 1000 | tf_op jit(solution)/shard_map/pallas_call | solution.py:351
  27.8 3.5 %shard_map.56 = (f32[4376,128]{1,0:T(8,128)S(1)}, f32[4376,128]{1,0:T(8,128)S(1)}, f32[1088,128]{1,0:T(8,128)S(1)}, f32[3104,128]{1,0:T(8,128)S(1)}, f32[128,128]{1,0:T(8,128)S(1)}) custom-call(f32[4376,128]{1,0:T(8,128)S(1)} %get-tuple-element.31.v_in, f32[4376,128]{1,0:T(8,128)S(1)} %get-tuple-element.32.f_in, ...), custom_call_target="tpu_custom_call", output_to_operand_aliasing={{0}: (0, {}), {1}: (1, {})} | custom-call | flops 20000000000 | bytes 1000 | tf_op jit(solution)/shard_map/pallas_call | solution.py:356
  31.2 0.0 collective-permute-done.2.above
  31.2 0.0 collective-permute-done.3.below
  31.2 1.3 %shard_map.57 = (f32[776,128]{1,0:T(8,128)S(1)}, f32[16,8,128]{2,1,0:T(8,128)S(1)}) custom-call(f32[416,128]{1,0:T(8,128)S(1)} %collective-permute-done.2.above, f32[416,128]{1,0:T(8,128)S(1)} %collective-permute-done.3.below, f32[4376,128]{1,0:T(8,128)S(1)} %get-tuple-element.35.v, f32[4376,128]{1,0:T(8,128)S(1)} %get-tuple-element.36.f, ...), custom_call_target="tpu_custom_call" | custom-call | flops 1000 | bytes 1000 | tf_op jit(solution)/shard_map/pallas_call | solution.py:364
  32.6 10.6 %all_to_all.5.got_ref = f32[16,8,128]{2,1,0:T(8,128)S(1)} all-to-all(f32[16,8,128]{2,1,0:T(8,128)S(1)} %get-tuple-element.39), channel_id=1, replica_groups=mesh['wrap'=32,'normal'=16] {'normal'}, dimensions={0} | all-to-all | bytes 131072 | tf_op jit(solution)/shard_map/all_to_all | solution.py:371
  43.2 1.2 %shard_map.58 = (bf16[96,32,128]{2,1,0:T(8,128)(2,1)}, f32[3,2,32]{2,1,0:T(2,128)}) custom-call(f32[16,8,128]{2,1,0:T(8,128)S(1)} %all_to_all.5.got_ref, f32[3104,128]{1,0:T(8,128)S(1)} %get-tuple-element.40.part, f32[776,128]{1,0:T(8,128)S(1)} %get-tuple-element.41.xe), custom_call_target="tpu_custom_call" | custom-call | flops 1000 | bytes 1000 | tf_op jit(solution)/shard_map/pallas_call | solution.py:372
  (3 shorter events, 0.1 us)
Async XLA Ops:
  2.8 9.8 %collective-permute-start = (f32[32,4,128]{2,1,0:T(4,128)S(1)}, f32[32,4,128]{2,1,0:T(4,128)S(1)}, u32[]{:S(2)}, u32[]{:S(2)}) collective-permute-start(f32[32,4,128]{2,1,0:T(4,128)S(1)} %get-tuple-element.23), channel_id=1, source_target_pairs={{1,2},{2,1},{3,4},{4,3},{5,6},{6,5},{7,8},{8,7},{9,10},{10,9},{11,... | collective-permute-start | bytes 196616 | tf_op jit(solution)/shard_map/ppermute | solution.py:344
  7.3 5.8 %collective-permute-start.1 = (f32[32,4,128]{2,1,0:T(4,128)S(1)}, f32[32,4,128]{2,1,0:T(4,128)S(1)}, u32[]{:S(2)}, u32[]{:S(2)}) collective-permute-start(f32[32,4,128]{2,1,0:T(4,128)S(1)} %shard_map.52.after_twin), channel_id=1, source_target_pairs={{0,1},{1,0},{2,3},{3,2},{4,5},{5,4},{6,7},{7,6},{8,9},{9,8},{10,11... | collective-permute-start | bytes 196616 | tf_op jit(solution)/shard_map/ppermute | solution.py:346
  13.2 18.0 %collective-permute-start.2 = (f32[416,128]{1,0:T(8,128)S(1)}, f32[416,128]{1,0:T(8,128)S(1)}, u32[]{:S(2)}, u32[]{:S(2)}) collective-permute-start(f32[416,128]{1,0:T(8,128)S(1)} %get-tuple-element.28), channel_id=1, source_target_pairs={{0,16},{16,32},{32,48},{48,64},{64,80},{80,96},{96,112},{112,128},... | collective-permute-start | bytes 638984 | tf_op jit(solution)/shard_map/ppermute | solution.py:354
  15.4 15.9 %collective-permute-start.3 = (f32[416,128]{1,0:T(8,128)S(1)}, f32[416,128]{1,0:T(8,128)S(1)}, u32[]{:S(2)}, u32[]{:S(2)}) collective-permute-start(f32[416,128]{1,0:T(8,128)S(1)} %get-tuple-element.29), channel_id=1, source_target_pairs={{16,0},{32,16},{48,32},{64,48},{80,64},{96,80},{112,96},{128,112},... | collective-permute-start | bytes 638984 | tf_op jit(solution)/shard_map/ppermute | solution.py:355

commit v7 on v6

--- a/solution.py
+++ b/solution.py
@@ -277,14 +277,14 @@
         chain(sweep + 1, coef_of(sweep) * value_of(sweep), line_of(kept, sweep))
         chain(3 * HALO - 1 - sweep, line_of(kept, HALO + sweep), None)
     sums[...] = sums_in[...]
-    eye = (iota((PLANES, COLS), 0) == iota((PLANES, COLS), 1)).astype(BF16)
     for k in range(2 * HALO):
         i = k if k < HALO else ROWS - 2 * HALO + k
         put_plain(plain, k, line_of(hv, HALO + k))
         high, p, q = line_sums(plain[pl.ds(k * WIDE, COLS), :], weight_of(weights[...], i))
         sums[pl.ds(i, 1), :] = p
         sums[pl.ds(ROWS + i, 1), :] = q
-        xe[pl.ds(k, PLANES, stride=2 * HALO), :] = nt(eye, high)
+        turned = jnp.transpose(high.astype(F32))[:PLANES]
+        xe[pl.ds(k, PLANES, stride=2 * HALO), :] = turned
     sums[...] = jnp.transpose(sums[...])
     owners = send_ref.shape[0]
     each = LAYER // owners

time: 44.7 us -> 44.5 us (level)
  no operation moved by 1% of the time
where the time goes in v7:
time: 44.5 us; the launch traced here: 44.3 us
  starting transfers between devices  22.4 us (50%)
  blocking collectives  10.6 us (24%)
  Pallas kernels  9.9 us (22%)
  between operations  0.74 us (2%)
  waiting for transfers between devices  0.56 us (1%)
    ppermute x1, starting transfers between devices, body(): lax.ppermute(top, 'wrap', [((k + 1) % wraps, k) for k in range(wraps)])  10.9 us
    all_to_all x1, blocking collectives, body(): got = lax.all_to_all(sums, 'normal', 0, 0, tiled=True)  10.6 us
    ppermute x1, starting transfers between devices, body(): twin = lax.ppermute(to_twin, 'normal', [(k, k ^ 1) for k in range(owners)])  4.94 us
    ppermute x1, starting transfers between devices, body(): lax.ppermute(to_cross, 'normal', [(k, k + 1 if k % 2 else k - 1) for k in...  4.51 us
    pallas_call x1, Pallas kernels, body(): call(inner_kernel, 5, [own_rows, own_rows, shaped(2 * HALO * WIDE, COLS),...  3.46 us
    pallas_call x1, Pallas kernels, body(): call(strip_kernel, [HBM] * 3, [shaped(ALL, COLS), strip, strip], [pltpu.V...  2.16 us
    ppermute x1, starting transfers between devices, body(): lax.ppermute(bottom, 'wrap', [(k, (k + 1) % wraps) for k in range(wraps)])  2.14 us
    pallas_call x1, Pallas kernels, body(): call(setup_kernel, 2, [own_rows, own_rows, square, square], [pltpu.VMEM((...  1.52 us
  transfers between devices with their start and end apart: 4, of which 1 were waited for; matrix products, arithmetic and copies ran while one was open for 0% of the time, Pallas kernels for 12%

profile of v7, /device:TPU:1, one launch (start us, length us, event | category | flops | bytes accessed | tf_op | source)
XLA Modules:
  0.0 44.3 jit_solution(9825407375629449242)
XLA Ops:
  0.6 2.2 %shard_map.50 = (f32[3136,128]{1,0:T(8,128)S(1)}, f32[32,4,128]{2,1,0:T(4,128)S(1)}, f32[32,4,128]{2,1,0:T(4,128)S(1)}) custom-call(bf16[96,32,128]{2,1,0:T(8,128)(2,1)} %bitcast.2, f32[32,128]{1,0:T(8,128)} %coef_hbm.1, f32[32,128]{1,0:T(8,128)} %spacing_hbm.1), custom_call_target="tpu_custom_call" | custom-call | flops 1000 | bytes 1000 | tf_op jit(solution)/shard_map/pallas_call | solution.py:336
  2.8 4.5 %collective-permute-start = (f32[32,4,128]{2,1,0:T(4,128)S(1)}, f32[32,4,128]{2,1,0:T(4,128)S(1)}, u32[]{:S(2)}, u32[]{:S(2)}) collective-permute-start(f32[32,4,128]{2,1,0:T(4,128)S(1)} %get-tuple-element.23), channel_id=1, source_target_pairs={{1,2},{2,1},{3,4},{4,3},{5,6},{6,5},{7,8},{8,7},{9,10},{10,9},{11,... | collective-permute-start | bytes 196616 | tf_op jit(solution)/shard_map/ppermute | solution.py:344
  7.3 4.9 %collective-permute-start.1 = (f32[32,4,128]{2,1,0:T(4,128)S(1)}, f32[32,4,128]{2,1,0:T(4,128)S(1)}, u32[]{:S(2)}, u32[]{:S(2)}) collective-permute-start(f32[32,4,128]{2,1,0:T(4,128)S(1)} %shard_map.52.after_twin), channel_id=1, source_target_pairs={{0,1},{1,0},{2,3},{3,2},{4,5},{5,4},{6,7},{7,6},{8,9},{9,8},{10,11... | collective-permute-start | bytes 196616 | tf_op jit(solution)/shard_map/ppermute | solution.py:346
  12.3 0.3 shard_map.53
  12.6 0.0 collective-permute-done.ref
  12.6 0.6 %collective-permute-done.1.twin = f32[32,4,128]{2,1,0:T(4,128)S(1)} collective-permute-done((f32[32,4,128]{2,1,0:T(4,128)S(1)}, f32[32,4,128]{2,1,0:T(4,128)S(1)}, u32[]{:S(2)}, u32[]{:S(2)}) %collective-permute-start.1) | collective-permute-done | bytes 65568 | tf_op jit(solution)/shard_map/ppermute | solution.py:346
  13.2 2.1 %collective-permute-start.2 = (f32[416,128]{1,0:T(8,128)S(1)}, f32[416,128]{1,0:T(8,128)S(1)}, u32[]{:S(2)}, u32[]{:S(2)}) collective-permute-start(f32[416,128]{1,0:T(8,128)S(1)} %get-tuple-element.28), channel_id=1, source_target_pairs={{0,16},{16,32},{32,48},{48,64},{64,80},{80,96},{96,112},{112,128},... | collective-permute-start | bytes 638984 | tf_op jit(solution)/shard_map/ppermute | solution.py:354
  15.4 10.9 %collective-permute-start.3 = (f32[416,128]{1,0:T(8,128)S(1)}, f32[416,128]{1,0:T(8,128)S(1)}, u32[]{:S(2)}, u32[]{:S(2)}) collective-permute-start(f32[416,128]{1,0:T(8,128)S(1)} %get-tuple-element.29), channel_id=1, source_target_pairs={{16,0},{32,16},{48,32},{64,48},{80,64},{96,80},{112,96},{128,112},... | collective-permute-start | bytes 638984 | tf_op jit(solution)/shard_map/ppermute | solution.py:355
  26.2 1.5 %shard_map.55 = (f32[4376,128]{1,0:T(8,128)S(1)}, f32[4376,128]{1,0:T(8,128)S(1)}, f32[128,128]{1,0:T(8,128)S(1)}, f32[128,128]{1,0:T(8,128)S(1)}) custom-call(f32[3136,128]{1,0:T(8,128)S(1)} %get-tuple-element.25.all_ref, f32[32,8,128]{2,1,0:T(8,128)S(1)} %get-tuple-element.30.after_corner.strips), custom_call_target="tpu_custom_call" | custom-call | flops 1000 | bytes 1000 | tf_op jit(solution)/shard_map/pallas_call | solution.py:351
  27.8 3.5 %shard_map.56 = (f32[4376,128]{1,0:T(8,128)S(1)}, f32[4376,128]{1,0:T(8,128)S(1)}, f32[1088,128]{1,0:T(8,128)S(1)}, f32[3104,128]{1,0:T(8,128)S(1)}, f32[128,128]{1,0:T(8,128)S(1)}) custom-call(f32[4376,128]{1,0:T(8,128)S(1)} %get-tuple-element.31.v_in, f32[4376,128]{1,0:T(8,128)S(1)} %get-tuple-element.32.f_in, ...), custom_call_target="tpu_custom_call", output_to_operand_aliasing={{0}: (0, {}), {1}: (1, {})} | custom-call | flops 20000000000 | bytes 1000 | tf_op jit(solution)/shard_map/pallas_call | solution.py:356
  31.2 0.0 collective-permute-done.2.above
  31.2 0.0 collective-permute-done.3.below
  31.2 1.2 %shard_map.57 = (f32[776,128]{1,0:T(8,128)S(1)}, f32[16,8,128]{2,1,0:T(8,128)S(1)}) custom-call(f32[416,128]{1,0:T(8,128)S(1)} %collective-permute-done.2.above, f32[416,128]{1,0:T(8,128)S(1)} %collective-permute-done.3.below, f32[4376,128]{1,0:T(8,128)S(1)} %get-tuple-element.35.v, f32[4376,128]{1,0:T(8,128)S(1)} %get-tuple-element.36.f, ...), custom_call_target="tpu_custom_call" | custom-call | flops 1000 | bytes 1000 | tf_op jit(solution)/shard_map/pallas_call | solution.py:364
  32.5 10.6 %all_to_all.5.got_ref = f32[16,8,128]{2,1,0:T(8,128)S(1)} all-to-all(f32[16,8,128]{2,1,0:T(8,128)S(1)} %get-tuple-element.39), channel_id=1, replica_groups=mesh['wrap'=32,'normal'=16] {'normal'}, dimensions={0} | all-to-all | bytes 131072 | tf_op jit(solution)/shard_map/all_to_all | solution.py:371
  43.1 1.2 %shard_map.58 = (bf16[96,32,128]{2,1,0:T(8,128)(2,1)}, f32[3,2,32]{2,1,0:T(2,128)}) custom-call(f32[16,8,128]{2,1,0:T(8,128)S(1)} %all_to_all.5.got_ref, f32[3104,128]{1,0:T(8,128)S(1)} %get-tuple-element.40.part, f32[776,128]{1,0:T(8,128)S(1)} %get-tuple-element.41.xe), custom_call_target="tpu_custom_call" | custom-call | flops 1000 | bytes 1000 | tf_op jit(solution)/shard_map/pallas_call | solution.py:372
  (3 shorter events, 0.1 us)
Async XLA Ops:
  2.8 9.8 %collective-permute-start = (f32[32,4,128]{2,1,0:T(4,128)S(1)}, f32[32,4,128]{2,1,0:T(4,128)S(1)}, u32[]{:S(2)}, u32[]{:S(2)}) collective-permute-start(f32[32,4,128]{2,1,0:T(4,128)S(1)} %get-tuple-element.23), channel_id=1, source_target_pairs={{1,2},{2,1},{3,4},{4,3},{5,6},{6,5},{7,8},{8,7},{9,10},{10,9},{11,... | collective-permute-start | bytes 196616 | tf_op jit(solution)/shard_map/ppermute | solution.py:344
  7.3 5.8 %collective-permute-start.1 = (f32[32,4,128]{2,1,0:T(4,128)S(1)}, f32[32,4,128]{2,1,0:T(4,128)S(1)}, u32[]{:S(2)}, u32[]{:S(2)}) collective-permute-start(f32[32,4,128]{2,1,0:T(4,128)S(1)} %shard_map.52.after_twin), channel_id=1, source_target_pairs={{0,1},{1,0},{2,3},{3,2},{4,5},{5,4},{6,7},{7,6},{8,9},{9,8},{10,11... | collective-permute-start | bytes 196616 | tf_op jit(solution)/shard_map/ppermute | solution.py:346
  13.2 18.0 %collective-permute-start.2 = (f32[416,128]{1,0:T(8,128)S(1)}, f32[416,128]{1,0:T(8,128)S(1)}, u32[]{:S(2)}, u32[]{:S(2)}) collective-permute-start(f32[416,128]{1,0:T(8,128)S(1)} %get-tuple-element.28), channel_id=1, source_target_pairs={{0,16},{16,32},{32,48},{48,64},{64,80},{80,96},{96,112},{112,128},... | collective-permute-start | bytes 638984 | tf_op jit(solution)/shard_map/ppermute | solution.py:354
  15.4 15.9 %collective-permute-start.3 = (f32[416,128]{1,0:T(8,128)S(1)}, f32[416,128]{1,0:T(8,128)S(1)}, u32[]{:S(2)}, u32[]{:S(2)}) collective-permute-start(f32[416,128]{1,0:T(8,128)S(1)} %get-tuple-element.29), channel_id=1, source_target_pairs={{16,0},{32,16},{48,32},{64,48},{80,64},{96,80},{112,96},{128,112},... | collective-permute-start | bytes 638984 | tf_op jit(solution)/shard_map/ppermute | solution.py:355

commit v8 on v6

--- a/solution.py
+++ b/solution.py
@@ -146,20 +146,20 @@
     for k in range(PARTS):
         piece = pl.ds(k * some, some)
         copies.append(pltpu.make_async_copy(x_hbm.at[piece], x_ref.at[piece], sems.at[k]))
-    for copy in copies[2:] + copies[:2]:
+    for copy in copies:
         copy.start()
+    copies[0].wait()
+    coef = all_ref[pl.ds(COEF_AT, ROWS), :]
+    coef_t = jnp.transpose(jnp.concatenate([coef, jnp.zeros((COLS - ROWS, COLS), F32)], axis=0))
+    ends = jnp.concatenate([coef_t[:HALO], coef_t[COLS - HALO :]], axis=0)
     for k in range(PARTS):
         copies[k + 2].wait()
         piece = x_ref[pl.ds(k * some, some)].astype(F32)
         all_ref[pl.ds(k * some * ROWS, some * ROWS), :] = piece.reshape(some * ROWS, COLS)
-    copies[0].wait()
     copies[1].wait()
     row, col = iota((2 * HALO, COLS), 0), iota((2 * HALO, COLS), 1)
     pick = (col == jnp.where(row < HALO, row, COLS - 2 * HALO + row)).astype(BF16)
     even = lax.axis_index("normal") % 2 == 0
-    coef = all_ref[pl.ds(COEF_AT, ROWS), :]
-    coef_t = jnp.transpose(jnp.concatenate([coef, jnp.zeros((COLS - ROWS, COLS), F32)], axis=0))
-    ends = jnp.concatenate([coef_t[:HALO], coef_t[COLS - HALO :]], axis=0)
     pad = jnp.zeros((COLS - PLANES, COLS), BF16)
     for i in range(ROWS):
         planes = all_ref[pl.ds(i, PLANES, stride=ROWS), :]

time: 44.7 us -> 44.8 us (level)
  no operation moved by 1% of the time
where the time goes in v8:
time: 44.8 us; the launch traced here: 44.4 us
  starting transfers between devices  22.4 us (50%)
  blocking collectives  10.6 us (24%)
  Pallas kernels  10.1 us (23%)
  between operations  0.74 us (2%)
  waiting for transfers between devices  0.56 us (1%)
    ppermute x1, starting transfers between devices, body(): lax.ppermute(top, 'wrap', [((k + 1) % wraps, k) for k in range(wraps)])  10.9 us
    all_to_all x1, blocking collectives, body(): got = lax.all_to_all(sums, 'normal', 0, 0, tiled=True)  10.6 us
    ppermute x1, starting transfers between devices, body(): twin = lax.ppermute(to_twin, 'normal', [(k, k ^ 1) for k in range(owners)])  4.94 us
    ppermute x1, starting transfers between devices, body(): lax.ppermute(to_cross, 'normal', [(k, k + 1 if k % 2 else k - 1) for k in...  4.51 us
    pallas_call x1, Pallas kernels, body(): call(inner_kernel, 5, [own_rows, own_rows, shaped(2 * HALO * WIDE, COLS),...  3.46 us
    pallas_call x1, Pallas kernels, body(): call(strip_kernel, [HBM] * 3, [shaped(ALL, COLS), strip, strip], [pltpu.V...  2.2 us
    ppermute x1, starting transfers between devices, body(): lax.ppermute(bottom, 'wrap', [(k, (k + 1) % wraps) for k in range(wraps)])  2.14 us
    pallas_call x1, Pallas kernels, body(): call(setup_kernel, 2, [own_rows, own_rows, square, square], [pltpu.VMEM((...  1.53 us
  transfers between devices with their start and end apart: 4, of which 1 were waited for; matrix products, arithmetic and copies ran while one was open for 0% of the time, Pallas kernels for 12%

profile of v8, /device:TPU:1, one launch (start us, length us, event | category | flops | bytes accessed | tf_op | source)
XLA Modules:
  0.0 44.4 jit_solution(7344353177708672669)
XLA Ops:
  0.6 2.2 %shard_map.50 = (f32[3136,128]{1,0:T(8,128)S(1)}, f32[32,4,128]{2,1,0:T(4,128)S(1)}, f32[32,4,128]{2,1,0:T(4,128)S(1)}) custom-call(bf16[96,32,128]{2,1,0:T(8,128)(2,1)} %bitcast.2, f32[32,128]{1,0:T(8,128)} %coef_hbm.1, f32[32,128]{1,0:T(8,128)} %spacing_hbm.1), custom_call_target="tpu_custom_call" | custom-call | flops 1000 | bytes 1000 | tf_op jit(solution)/shard_map/pallas_call | solution.py:336
  2.8 4.5 %collective-permute-start = (f32[32,4,128]{2,1,0:T(4,128)S(1)}, f32[32,4,128]{2,1,0:T(4,128)S(1)}, u32[]{:S(2)}, u32[]{:S(2)}) collective-permute-start(f32[32,4,128]{2,1,0:T(4,128)S(1)} %get-tuple-element.23), channel_id=1, source_target_pairs={{1,2},{2,1},{3,4},{4,3},{5,6},{6,5},{7,8},{8,7},{9,10},{10,9},{11,... | collective-permute-start | bytes 196616 | tf_op jit(solution)/shard_map/ppermute | solution.py:344
  7.4 4.9 %collective-permute-start.1 = (f32[32,4,128]{2,1,0:T(4,128)S(1)}, f32[32,4,128]{2,1,0:T(4,128)S(1)}, u32[]{:S(2)}, u32[]{:S(2)}) collective-permute-start(f32[32,4,128]{2,1,0:T(4,128)S(1)} %shard_map.52.after_twin), channel_id=1, source_target_pairs={{0,1},{1,0},{2,3},{3,2},{4,5},{5,4},{6,7},{7,6},{8,9},{9,8},{10,11... | collective-permute-start | bytes 196616 | tf_op jit(solution)/shard_map/ppermute | solution.py:346
  12.3 0.3 shard_map.53
  12.6 0.0 collective-permute-done.ref
  12.6 0.6 %collective-permute-done.1.twin = f32[32,4,128]{2,1,0:T(4,128)S(1)} collective-permute-done((f32[32,4,128]{2,1,0:T(4,128)S(1)}, f32[32,4,128]{2,1,0:T(4,128)S(1)}, u32[]{:S(2)}, u32[]{:S(2)}) %collective-permute-start.1) | collective-permute-done | bytes 65568 | tf_op jit(solution)/shard_map/ppermute | solution.py:346
  13.2 2.1 %collective-permute-start.2 = (f32[416,128]{1,0:T(8,128)S(1)}, f32[416,128]{1,0:T(8,128)S(1)}, u32[]{:S(2)}, u32[]{:S(2)}) collective-permute-start(f32[416,128]{1,0:T(8,128)S(1)} %get-tuple-element.28), channel_id=1, source_target_pairs={{0,16},{16,32},{32,48},{48,64},{64,80},{80,96},{96,112},{112,128},... | collective-permute-start | bytes 638984 | tf_op jit(solution)/shard_map/ppermute | solution.py:354
  15.4 10.9 %collective-permute-start.3 = (f32[416,128]{1,0:T(8,128)S(1)}, f32[416,128]{1,0:T(8,128)S(1)}, u32[]{:S(2)}, u32[]{:S(2)}) collective-permute-start(f32[416,128]{1,0:T(8,128)S(1)} %get-tuple-element.29), channel_id=1, source_target_pairs={{16,0},{32,16},{48,32},{64,48},{80,64},{96,80},{112,96},{128,112},... | collective-permute-start | bytes 638984 | tf_op jit(solution)/shard_map/ppermute | solution.py:355
  26.3 1.5 %shard_map.55 = (f32[4376,128]{1,0:T(8,128)S(1)}, f32[4376,128]{1,0:T(8,128)S(1)}, f32[128,128]{1,0:T(8,128)S(1)}, f32[128,128]{1,0:T(8,128)S(1)}) custom-call(f32[3136,128]{1,0:T(8,128)S(1)} %get-tuple-element.25.all_ref, f32[32,8,128]{2,1,0:T(8,128)S(1)} %get-tuple-element.30.after_corner.strips), custom_call_target="tpu_custom_call" | custom-call | flops 1000 | bytes 1000 | tf_op jit(solution)/shard_map/pallas_call | solution.py:351
  27.8 3.5 %shard_map.56 = (f32[4376,128]{1,0:T(8,128)S(1)}, f32[4376,128]{1,0:T(8,128)S(1)}, f32[1088,128]{1,0:T(8,128)S(1)}, f32[3104,128]{1,0:T(8,128)S(1)}, f32[128,128]{1,0:T(8,128)S(1)}) custom-call(f32[4376,128]{1,0:T(8,128)S(1)} %get-tuple-element.31.v_in, f32[4376,128]{1,0:T(8,128)S(1)} %get-tuple-element.32.f_in, ...), custom_call_target="tpu_custom_call", output_to_operand_aliasing={{0}: (0, {}), {1}: (1, {})} | custom-call | flops 20000000000 | bytes 1000 | tf_op jit(solution)/shard_map/pallas_call | solution.py:356
  31.2 0.0 collective-permute-done.2.above
  31.3 0.0 collective-permute-done.3.below
  31.3 1.3 %shard_map.57 = (f32[776,128]{1,0:T(8,128)S(1)}, f32[16,8,128]{2,1,0:T(8,128)S(1)}) custom-call(f32[416,128]{1,0:T(8,128)S(1)} %collective-permute-done.2.above, f32[416,128]{1,0:T(8,128)S(1)} %collective-permute-done.3.below, f32[4376,128]{1,0:T(8,128)S(1)} %get-tuple-element.35.v, f32[4376,128]{1,0:T(8,128)S(1)} %get-tuple-element.36.f, ...), custom_call_target="tpu_custom_call" | custom-call | flops 1000 | bytes 1000 | tf_op jit(solution)/shard_map/pallas_call | solution.py:364
  32.6 10.6 %all_to_all.5.got_ref = f32[16,8,128]{2,1,0:T(8,128)S(1)} all-to-all(f32[16,8,128]{2,1,0:T(8,128)S(1)} %get-tuple-element.39), channel_id=1, replica_groups=mesh['wrap'=32,'normal'=16] {'normal'}, dimensions={0} | all-to-all | bytes 131072 | tf_op jit(solution)/shard_map/all_to_all | solution.py:371
  43.3 1.2 %shard_map.58 = (bf16[96,32,128]{2,1,0:T(8,128)(2,1)}, f32[3,2,32]{2,1,0:T(2,128)}) custom-call(f32[16,8,128]{2,1,0:T(8,128)S(1)} %all_to_all.5.got_ref, f32[3104,128]{1,0:T(8,128)S(1)} %get-tuple-element.40.part, f32[776,128]{1,0:T(8,128)S(1)} %get-tuple-element.41.xe), custom_call_target="tpu_custom_call" | custom-call | flops 1000 | bytes 1000 | tf_op jit(solution)/shard_map/pallas_call | solution.py:372
  (3 shorter events, 0.1 us)
Async XLA Ops:
  2.8 9.8 %collective-permute-start = (f32[32,4,128]{2,1,0:T(4,128)S(1)}, f32[32,4,128]{2,1,0:T(4,128)S(1)}, u32[]{:S(2)}, u32[]{:S(2)}) collective-permute-start(f32[32,4,128]{2,1,0:T(4,128)S(1)} %get-tuple-element.23), channel_id=1, source_target_pairs={{1,2},{2,1},{3,4},{4,3},{5,6},{6,5},{7,8},{8,7},{9,10},{10,9},{11,... | collective-permute-start | bytes 196616 | tf_op jit(solution)/shard_map/ppermute | solution.py:344
  7.4 5.8 %collective-permute-start.1 = (f32[32,4,128]{2,1,0:T(4,128)S(1)}, f32[32,4,128]{2,1,0:T(4,128)S(1)}, u32[]{:S(2)}, u32[]{:S(2)}) collective-permute-start(f32[32,4,128]{2,1,0:T(4,128)S(1)} %shard_map.52.after_twin), channel_id=1, source_target_pairs={{0,1},{1,0},{2,3},{3,2},{4,5},{5,4},{6,7},{7,6},{8,9},{9,8},{10,11... | collective-permute-start | bytes 196616 | tf_op jit(solution)/shard_map/ppermute | solution.py:346
  13.2 18.0 %collective-permute-start.2 = (f32[416,128]{1,0:T(8,128)S(1)}, f32[416,128]{1,0:T(8,128)S(1)}, u32[]{:S(2)}, u32[]{:S(2)}) collective-permute-start(f32[416,128]{1,0:T(8,128)S(1)} %get-tuple-element.28), channel_id=1, source_target_pairs={{0,16},{16,32},{32,48},{48,64},{64,80},{80,96},{96,112},{112,128},... | collective-permute-start | bytes 638984 | tf_op jit(solution)/shard_map/ppermute | solution.py:354
  15.4 15.9 %collective-permute-start.3 = (f32[416,128]{1,0:T(8,128)S(1)}, f32[416,128]{1,0:T(8,128)S(1)}, u32[]{:S(2)}, u32[]{:S(2)}) collective-permute-start(f32[416,128]{1,0:T(8,128)S(1)} %get-tuple-element.29), channel_id=1, source_target_pairs={{16,0},{32,16},{48,32},{64,48},{80,64},{96,80},{112,96},{128,112},... | collective-permute-start | bytes 638984 | tf_op jit(solution)/shard_map/ppermute | solution.py:355
